TPU v7x, 256 devices: a whole 4x4x8 slice. The times are simulated.
256 devices in a mesh: blk: 4 (over x), seq: 16 (over z, core), tensor: 4 (over y).
Axes of the slice: x: 4, y: 4, z: 8, core: 2. Of those that a mesh axis runs over, the one named last changes fastest.
Arguments:
- tokens: bfloat16 [4, 4096, 4096], P('blk', 'seq', 'tensor'), may hold values from -20 to 20
- w_query: bfloat16 [4, 4096, 2048], P('blk', 'seq', 'tensor'), may hold values from -0.09375 to 0.09375
- w_keyval: bfloat16 [4, 4096, 4, 256], P('blk', 'seq', 'tensor'), may hold values from -0.09375 to 0.09375
- accum_query: float32 [4, 4096, 2048], P('blk', 'seq', 'tensor'), may hold values from -0.75 to 0.75
- accum_keyval: float32 [4, 4096, 4, 256], P('blk', 'seq', 'tensor'), may hold values from -0.75 to 0.75
- cotangent: bfloat16 [4, 4096, 2048], P('blk', 'seq', 'tensor'), may hold values from -6 to 6
- seg_ids: int32 [4, 4096], P('blk'), may hold values from 0 to 7, never falling along the last dimension, each value on 1 to 2048 neighbouring positions
- spans: int32 [4, 8, 2], P('blk'), may hold values from 0 to 4096, as said below
- counts: int32 [4, 16], P('blk'), may hold values from 128 to 256, as said below
Outputs:
- context: bfloat16 [4, 4096, 2048], P('blk', 'seq', 'tensor')
- grad_tokens: bfloat16 [4, 4096, 4096], P('blk', 'seq', 'tensor')
- accum_query_out: float32 [4, 4096, 2048], P('blk', 'seq', 'tensor')
- accum_keyval_out: float32 [4, 4096, 4, 256], P('blk', 'seq', 'tensor')
Inputs may be any that keep to these rules, and one draw needn't show every extreme that they name: `spans`: start < end for every document slot; some slot starts at 0 and some ends at 4096 in every micro-batch. `counts`: in every micro-batch some index of seq is full.
All inputs are finite; a program needn't handle non-finite values.
Results may differ from a plain program's by a relative error of at most 0.011.
Values may be sent and summed in bfloat16 or wider, within the bound.
A program may use at most 128 MiB of HBM per device.

v0:
```python
import jax
import jax.numpy as jnp
from jax import lax
from jax.sharding import PartitionSpec as P


def passed_along(block, axis, distance):
    devices = range(lax.axis_size(axis))
    route = [((i - distance) % len(devices), i) for i in devices]
    return lax.ppermute(block, axis, route)


def on_device(
    tokens, w_query, w_keyval, accum_query, accum_keyval, cotangent, seg_ids, spans, counts
):
    rank = lax.axis_index("seq")
    full = lax.all_gather(tokens, "tensor", axis=2, tiled=True)[0]
    rows = full.shape[0]
    moved_q, moved_kv = passed_along((w_query, w_keyval), "blk", 1)
    groups = moved_kv.shape[2]
    headsz = moved_kv.shape[3] // 2
    qcols = moved_q.shape[2]
    kcols = groups * 2 * headsz
    query_per_group = qcols // (groups * headsz)
    part_w = jnp.concatenate([moved_q[0], moved_kv[0].reshape(moved_kv.shape[1], kcols)], axis=1)
    whole_w = lax.all_gather(part_w, "seq", axis=0, tiled=True)
    projected = jnp.dot(full, whole_w, preferred_element_type=jnp.float32)
    lowered = projected.astype(jnp.bfloat16)
    query = lowered[:, :qcols].reshape(rows, groups, query_per_group, headsz)
    keyval = lowered[:, qcols:]
    all_kv = lax.all_gather(keyval, "seq", axis=0, tiled=True)
    total = all_kv.shape[0]
    kv_heads = all_kv.reshape(total, groups, 2 * headsz)
    keys = kv_heads[:, :, :headsz]
    value_rows = kv_heads[:, :, headsz:]
    segs = seg_ids[0]
    span = spans[0]
    cnt = counts[0]
    kpos = jnp.arange(total, dtype=jnp.int32)
    qpos = rank * rows + jnp.arange(rows, dtype=jnp.int32)
    owner = jnp.repeat(cnt, rows, total_repeat_length=total)
    kvalid = kpos % rows < owner
    onehot = segs[:, None] == jnp.arange(span.shape[0], dtype=jnp.int32)[None, :]
    first = jnp.sum(jnp.where(onehot, span[None, :, 0], 0), axis=1)
    last = jnp.sum(jnp.where(onehot, span[None, :, 1], 0), axis=1)
    kinside = (kpos >= first) & (kpos < last)
    query_validity_mask = lax.dynamic_slice_in_dim(kvalid, rank * rows, rows)
    qinside = lax.dynamic_slice_in_dim(kinside, rank * rows, rows)
    qseg = lax.dynamic_slice_in_dim(segs, rank * rows, rows)
    allowed = (
        (qseg[:, None] == segs[None, :])
        & ((kpos[None, :] <= qpos[:, None]) | qinside[:, None] & kinside[None, :])
        & kvalid[None, :]
    )
    allowed = allowed | (kpos[None, :] == qpos[:, None])
    scale = headsz ** (-0.5)
    scores = jnp.einsum("igxd,jgd->gxij", query, keys, preferred_element_type=jnp.float32) * scale
    scores = jnp.where(allowed[None, None], scores, -jnp.inf)
    top = jnp.max(scores, axis=-1, keepdims=True)
    expo = jnp.exp(scores - top)
    probs = expo / jnp.sum(expo, axis=-1, keepdims=True)
    probability_lowprec = probs.astype(jnp.bfloat16)
    value_mask = query_validity_mask.astype(jnp.float32)[:, None, None, None]
    attended_output = (
        jnp.einsum(
            "zcft,tzn->fzcn", probability_lowprec, value_rows, preferred_element_type=jnp.float32
        )
        * value_mask
    )
    context = attended_output.reshape(rows, qcols).astype(jnp.bfloat16)
    upstream_gradient = jnp.where(
        query_validity_mask[:, None, None, None],
        cotangent[0].reshape(rows, groups, query_per_group, headsz),
        jnp.zeros((), jnp.bfloat16),
    )
    delta = jnp.transpose(
        jnp.sum(upstream_gradient.astype(jnp.float32) * attended_output, axis=-1), (1, 2, 0)
    )
    dprobs = jnp.einsum(
        "igxd,jgd->gxij", upstream_gradient, value_rows, preferred_element_type=jnp.float32
    )
    dscores = (probs * (dprobs - delta[..., None]) * scale).astype(jnp.bfloat16)
    dquery = (
        jnp.einsum("zcft,tzn->fzcn", dscores, keys, preferred_element_type=jnp.float32)
        .astype(jnp.bfloat16)
        .reshape(rows, qcols)
    )
    dkey = jnp.einsum("gxij,igxd->jgd", dscores, query, preferred_element_type=jnp.float32)
    dval = jnp.einsum(
        "gxij,igxd->jgd", probability_lowprec, upstream_gradient, preferred_element_type=jnp.float32
    )
    dkv_terms = jnp.concatenate([dkey, dval], axis=-1).reshape(total, kcols)
    dkeyval = lax.psum_scatter(dkv_terms, "seq", scatter_dimension=0, tiled=True).astype(
        jnp.bfloat16
    )
    dprojected = jnp.concatenate([dquery, dkeyval], axis=1)
    partial_x = jnp.einsum("ic,dc->id", dprojected, whole_w, preferred_element_type=jnp.float32)
    grad_tokens = lax.psum_scatter(partial_x, "tensor", scatter_dimension=1, tiled=True).astype(
        jnp.bfloat16
    )
    fresh = lax.psum_scatter(
        jnp.einsum("ic,ie->ce", full, dprojected, preferred_element_type=jnp.float32) / total,
        "seq",
        scatter_dimension=0,
        tiled=True,
    )
    arrived = passed_along(fresh, "blk", -1)
    cycle_q, cycle_kv = passed_along((accum_query, accum_keyval), "blk", 1)
    out_q = cycle_q + arrived[:, :qcols][None]
    out_kv = cycle_kv + arrived[:, qcols:].reshape(1, arrived.shape[0], groups, 2 * headsz)
    return (context[None], grad_tokens[None], out_q, out_kv)


def solution(mesh):
    in_specs = (
        P("blk", "seq", "tensor"),
        P("blk", "seq", "tensor"),
        P("blk", "seq", "tensor", None),
        P("blk", "seq", "tensor"),
        P("blk", "seq", "tensor", None),
        P("blk", "seq", "tensor"),
        P("blk", None),
        P("blk", None, None),
        P("blk", None),
    )
    out_specs = (
        P("blk", "seq", "tensor"),
        P("blk", "seq", "tensor"),
        P("blk", "seq", "tensor"),
        P("blk", "seq", "tensor", None),
    )
    return jax.shard_map(
        on_device, mesh=mesh, in_specs=in_specs, out_specs=out_specs, check_vma=False
    )
```

profile of v0, /device:TPU:6, one launch (start us, length us, event | category | flops | bytes accessed | tf_op | source)
XLA Modules:
  0.0 388.9 jit_solution(15031069585912791990)
XLA Ops:
  8.2 2.3 collective-permute-start
  10.6 8.8 %collective-permute-done.1 = bf16[1,256,1,256]{3,1,2,0:T(8,128)(2,1)S(1)} collective-permute-done((bf16[1,256,1,256]{3,1,2,0:T(8,128)(2,1)}, bf16[1,256,1,256]{3,1,2,0:T(8,128)(2,1)S(1)}, u32[]{:S(2)}, u32[]{:S(2)}) %collective-permute-start.1) | collective-permute-done | bytes 131104 | tf_op jit(solution)/shard_map/ppermute | solution.py:10
  20.2 26.2 %all-gather.6.cloned.1.call-done = bf16[1,256,4096]{2,1,0:T(8,128)(2,1)} async-done(((bf16[1,256,1024]{2,1,0:T(8,128)(2,1)}), bf16[1,256,4096]{2,1,0:T(8,128)(2,1)}) %all-gather.6.cloned.1.call-update) | async-done | bytes 2097168 | tf_op jit(solution)/shard_map/all_gather | solution.py:17
  46.4 48.5 %all-gather.4.cloned.1.call-done = bf16[4096,768]{1,0:T(8,128)(2,1)} async-done(((bf16[256,768]{1,0:T(8,128)(2,1)}), bf16[4096,768]{1,0:T(8,128)(2,1)}) %all-gather.4.cloned.1.call-update) | async-done | bytes 6291472 | tf_op jit(solution)/shard_map/all_gather | solution.py:26
  94.9 5.2 %fusion.43 = bf16[256,768]{0,1:T(8,128)(2,1)S(1)} fusion(bf16[4096,768]{1,0:T(8,128)(2,1)} %all-gather.4.cloned.1.call-done, bf16[1,256,4096]{2,1,0:T(8,128)(2,1)} %all-gather.6.cloned.1.call-done), kind=kOutput, calls=%fused_computation.36 | convolution fusion | flops 1610809344 | bytes 8781824 | tf_op jit(solution)/shard_map/dot_general | solution.py:27
  102.9 10.0 %fusion.54 = pred[4096]{0:T(1024)(128)(4,1)S(1)} fusion(pred[4096]{0:T(1024)(128)(4,1)S(1)} %copy-done.9, pred[4096]{0:T(1024)(128)(4,1)S(1)} %copy-done.10, pred[4096]{0:T(1024)(128)(4,1)S(1)} %copy-done.11, pred[4096]{0:T(1024)(128)(4,1)S(1)} %copy-done.12, pred[4096]{0:T(1024)(128)(4,1)S(1)} %copy-done.13, pred[4096]{0:T(1024)(128)(4,1)S(1)} %copy-done.14, ...), kind=kLoop, calls=%fused_computation.58 | loop fusion | flops 90112 | bytes 65600 | tf_op jit(solution)/shard_map/lt | solution.py:42
  114.3 3.6 fusion.24
  118.6 22.0 %all-gather.8.cloned.1.call-done = bf16[4096,256]{0,1:T(8,128)(2,1)} async-done(((bf16[256,256]{0,1:T(8,128)(2,1)}), bf16[4096,256]{0,1:T(8,128)(2,1)}) %all-gather.8.cloned.1.call-update) | async-done | bytes 2097168 | tf_op jit(solution)/shard_map/all_gather | solution.py:31
  140.6 4.1 %fusion.5 = (f32[4,256]{1,0:T(4,128)S(1)}, f32[4096,256,4]{1,0,2:T(8,128)S(1)}) fusion(pred[256,4096]{0,1:T(8,128)(4,1)S(1)} %fusion.24, bf16[256,4,128]{0,2,1:T(8,128)(2,1)} %bitcast.161, bf16[4096,1,256]{0,2,1:T(8,128)(2,1)} %bitcast.174), kind=kOutput, calls=%fused_computation.8 | convolution fusion | flops 1086323712 | bytes 19140608 | tf_op jit(solution)/shard_map/igxd,jgd->gxij/dot_general | solution.py:57
  144.7 3.6 fusion.4
  148.3 6.5 %fusion.15 = f32[4096,1,128]{0,2,1:T(8,128)} fusion(bf16[256,4,128]{0,2,1:T(8,128)(2,1)S(1)} %bitcast.166, pred[256]{0:T(512)(128)(4,1)S(1)} %get-tuple-element.27, f32[4,256]{1,0:T(4,128)S(1)} %fusion.4, f32[4,256]{1,0:T(4,128)S(1)} %get-tuple-element.48, f32[4096,256,4]{1,0,2:T(8,128)S(1)} %get-tuple-element.49, pred[256,4096]{0,1:T(8,128)(4,1)S(1)} %fusion.24), kind=kOutput, calls=%fused_computation.19 | convolution fusion | flops 1094844416 | bytes 20193536 | tf_op jit(solution)/shard_map/gxij,igxd->jgd/dot_general | solution.py:89
  154.9 6.2 %multiply_reduce_fusion = (f32[256,4]{0,1:T(4,128)}, bf16[256,1,4,128]{0,3,2,1:T(8,128)(2,1)}) fusion(bf16[256,1,4,128]{0,3,2,1:T(8,128)(2,1)S(1)} %bitcast.167, pred[256]{0:T(512)(128)(4,1)S(1)} %get-tuple-element.27, f32[256]{0:T(256)S(1)} %copy-done.25, f32[4,256]{1,0:T(4,128)S(1)} %fusion.4, f32[4,256]{1,0:T(4,128)S(1)} %get-tuple-element.48, ...), kind=kOutput, calls=%fused_computation.43 | convolution fusion | flops 1095498752 | bytes 19412480 | tf_op jit(solution)/shard_map/zcft,tzn->fzcn/dot_general | solution.py:65
  161.1 9.5 %fusion.2 = bf16[1,4,256,4096]{2,3,1,0:T(8,128)(2,1)} fusion(f32[4,256]{1,0:T(4,128)} %bitcast.178, f32[4,256]{1,0:T(4,128)S(1)} %fusion.4, f32[4,256]{1,0:T(4,128)S(1)} %get-tuple-element.48, f32[4096,256,4]{1,0,2:T(8,128)S(1)} %get-tuple-element.49, pred[256,4096]{0,1:T(8,128)(4,1)S(1)} %fusion.24, bf16[4096,1,256]{0,2,1:T(8,128)(2,1)} %bitcast.175, ...), kind=kOutput, calls=%fused_computation.3 | convolution fusion | flops 1107296256 | bytes 27537408 | tf_op jit(solution)/shard_map/igxd,jgd->gxij/dot_general | solution.py:79
  170.7 6.4 %fusion.18 = f32[4096,1,128]{0,2,1:T(8,128)S(1)} fusion(bf16[256,4,128]{0,2,1:T(8,128)(2,1)} %bitcast.162, bf16[1,4,256,4096]{2,3,1,0:T(8,128)(2,1)} %fusion.2), kind=kOutput, calls=%fused_computation.20 | convolution fusion | flops 1073741824 | bytes 10747904 | tf_op jit(solution)/shard_map/gxij,igxd->jgd/dot_general | solution.py:88
  177.1 2.3 maximum_bitcast_fusion
  179.4 5.1 %fusion.40 = bf16[128,4,256]{2,0,1:T(8,128)(2,1)S(1)} fusion(bf16[1,4,256,4096]{2,3,1,0:T(8,128)(2,1)} %fusion.2, bf16[4096,1,256]{0,2,1:T(8,128)(2,1)} %bitcast.176), kind=kOutput, calls=%fused_computation.35 | convolution fusion | flops 1073872896 | bytes 9699328 | tf_op jit(solution)/shard_map/zcft,tzn->fzcn/dot_general | solution.py:84
  184.5 57.0 %reduce-scatter.4.cloned.1.call-done = f32[256,256]{0,1:T(8,128)} async-done(((f32[4096,256]{0,1:T(8,128)}), f32[256,256]{0,1:T(8,128)}) %reduce-scatter.4.cloned.1.call-update) | async-done | bytes 262160 | tf_op jit(solution)/shard_map/reduce_scatter | solution.py:93
  242.5 6.3 %multiply_bitcast_fusion = f32[4096,768]{0,1:T(8,128)} fusion(bf16[1,256,4096]{2,1,0:T(8,128)(2,1)S(1)} %copy-done, bf16[256,256]{0,1:T(8,128)(2,1)S(1)} %convert_element_type.65, bf16[256,512]{0,1:T(8,128)(2,1)S(1)} %bitcast.163), kind=kOutput, calls=%fused_computation.9 | convolution fusion | flops 1614544896 | bytes 15073280 | tf_op jit(solution)/shard_map/ic,ie->ce/dot_general | solution.py:102
  249.0 6.7 %fusion.52 = f32[256,4096]{1,0:T(8,128)} fusion(bf16[4096,768]{1,0:T(8,128)(2,1)} %all-gather.4.cloned.1.call-done, bf16[256,256]{0,1:T(8,128)(2,1)S(1)} %convert_element_type.65, bf16[256,512]{0,1:T(8,128)(2,1)S(1)} %bitcast.164), kind=kOutput, calls=%fused_computation.52 | convolution fusion | flops 1611399168 | bytes 10878976 | tf_op jit(solution)/shard_map/ic,dc->id/dot_general | solution.py:97
  255.7 71.1 %reduce-scatter.8.cloned.1.call-done = f32[256,768]{0,1:T(8,128)} async-done(((f32[4096,768]{0,1:T(8,128)}), f32[256,768]{0,1:T(8,128)}) %reduce-scatter.8.cloned.1.call-update) | async-done | bytes 786448 | tf_op jit(solution)/shard_map/reduce_scatter | solution.py:101
  327.9 2.4 collective-permute-start.2
  331.4 46.6 %reduce-scatter.6.cloned.1.call-done = f32[256,1024]{1,0:T(8,128)} async-done(((f32[256,4096]{1,0:T(8,128)}), f32[256,1024]{1,0:T(8,128)}) %reduce-scatter.6.cloned.1.call-update) | async-done | bytes 1048592 | tf_op jit(solution)/shard_map/reduce_scatter | solution.py:98
  378.0 2.1 convert_bitcast_fusion
  380.2 1.0 copy.41
  (94 shorter events, 10.7 us)
Async XLA Ops:
  7.2 95.5 %copy-start.9 = (pred[4096]{0:T(1024)(128)(4,1)S(1)}, pred[4096]{0:T(1024)(128)(4,1)}, u32[]{:S(2)}) copy-start(pred[4096]{0:T(1024)(128)(4,1)} %constant.167) | copy-start | bytes 12292
  7.2 95.5 %copy-start.10 = (pred[4096]{0:T(1024)(128)(4,1)S(1)}, pred[4096]{0:T(1024)(128)(4,1)}, u32[]{:S(2)}) copy-start(pred[4096]{0:T(1024)(128)(4,1)} %constant.168) | copy-start | bytes 12292
  7.2 95.5 %copy-start.11 = (pred[4096]{0:T(1024)(128)(4,1)S(1)}, pred[4096]{0:T(1024)(128)(4,1)}, u32[]{:S(2)}) copy-start(pred[4096]{0:T(1024)(128)(4,1)} %constant.169) | copy-start | bytes 12292
  7.2 95.5 %copy-start.12 = (pred[4096]{0:T(1024)(128)(4,1)S(1)}, pred[4096]{0:T(1024)(128)(4,1)}, u32[]{:S(2)}) copy-start(pred[4096]{0:T(1024)(128)(4,1)} %constant.170) | copy-start | bytes 12292
  7.2 95.5 %copy-start.13 = (pred[4096]{0:T(1024)(128)(4,1)S(1)}, pred[4096]{0:T(1024)(128)(4,1)}, u32[]{:S(2)}) copy-start(pred[4096]{0:T(1024)(128)(4,1)} %constant.171) | copy-start | bytes 12292
  7.2 95.5 %copy-start.14 = (pred[4096]{0:T(1024)(128)(4,1)S(1)}, pred[4096]{0:T(1024)(128)(4,1)}, u32[]{:S(2)}) copy-start(pred[4096]{0:T(1024)(128)(4,1)} %constant.172) | copy-start | bytes 12292
  7.2 95.5 %copy-start.15 = (pred[4096]{0:T(1024)(128)(4,1)S(1)}, pred[4096]{0:T(1024)(128)(4,1)}, u32[]{:S(2)}) copy-start(pred[4096]{0:T(1024)(128)(4,1)} %constant.173) | copy-start | bytes 12292
  7.3 95.5 %copy-start.16 = (pred[4096]{0:T(1024)(128)(4,1)S(1)}, pred[4096]{0:T(1024)(128)(4,1)}, u32[]{:S(2)}) copy-start(pred[4096]{0:T(1024)(128)(4,1)} %constant.174) | copy-start | bytes 12292
  7.3 95.5 %copy-start.17 = (pred[4096]{0:T(1024)(128)(4,1)S(1)}, pred[4096]{0:T(1024)(128)(4,1)}, u32[]{:S(2)}) copy-start(pred[4096]{0:T(1024)(128)(4,1)} %constant.175) | copy-start | bytes 12292
  7.3 95.5 %copy-start.18 = (pred[4096]{0:T(1024)(128)(4,1)S(1)}, pred[4096]{0:T(1024)(128)(4,1)}, u32[]{:S(2)}) copy-start(pred[4096]{0:T(1024)(128)(4,1)} %constant.176) | copy-start | bytes 12292
  7.3 95.5 %copy-start.19 = (pred[4096]{0:T(1024)(128)(4,1)S(1)}, pred[4096]{0:T(1024)(128)(4,1)}, u32[]{:S(2)}) copy-start(pred[4096]{0:T(1024)(128)(4,1)} %constant.177) | copy-start | bytes 12292
  7.3 95.5 %copy-start.20 = (pred[4096]{0:T(1024)(128)(4,1)S(1)}, pred[4096]{0:T(1024)(128)(4,1)}, u32[]{:S(2)}) copy-start(pred[4096]{0:T(1024)(128)(4,1)} %constant.178) | copy-start | bytes 12292
  7.3 95.5 %copy-start.21 = (pred[4096]{0:T(1024)(128)(4,1)S(1)}, pred[4096]{0:T(1024)(128)(4,1)}, u32[]{:S(2)}) copy-start(pred[4096]{0:T(1024)(128)(4,1)} %constant.179) | copy-start | bytes 12292
  7.4 39.0 %all-gather.6.cloned.1.call-start = ((), (), s32[]{:S(2)}) async-start(), calls=%async_computation.4 | async-start | bytes 2621440 | tf_op jit(solution)/shard_map/all_gather | solution.py:17
  8.1 86.8 %all-gather.4.cloned.1.call-start = ((), (), s32[]{:S(2)}) async-start(), calls=%async_computation.3 | async-start | bytes 6684672 | tf_op jit(solution)/shard_map/all_gather | solution.py:26
  8.2 11.1 %collective-permute-start = (bf16[1,256,512]{2,1,0:T(8,128)(2,1)}, bf16[1,256,512]{2,1,0:T(8,128)(2,1)S(1)}, u32[]{:S(2)}, u32[]{:S(2)}) collective-permute-start(bf16[1,256,512]{2,1,0:T(8,128)(2,1)} %param.12), channel_id=1, source_target_pairs={{192,0},{0,64},{64,128},{128,192},{193,1},{1,65},{65,129},{129,193... | collective-permute-start | bytes 786440 | tf_op jit(solution)/shard_map/ppermute | solution.py:10
  10.5 8.9 %collective-permute-start.1 = (bf16[1,256,1,256]{3,1,2,0:T(8,128)(2,1)}, bf16[1,256,1,256]{3,1,2,0:T(8,128)(2,1)S(1)}, u32[]{:S(2)}, u32[]{:S(2)}) collective-permute-start(bf16[1,256,1,256]{3,1,2,0:T(8,128)(2,1)} %param.13), channel_id=1, source_target_pairs={{192,0},{0,64},{64,128},{128,192},{193,1},{1,65},{65,129},{129,193... | collective-permute-start | bytes 393224 | tf_op jit(solution)/shard_map/ppermute | solution.py:10
  20.1 120.4 %all-gather.8.cloned.1.call-start = ((), (), s32[]{:S(2)}) async-start(), calls=%async_computation.5 | async-start | bytes 2228224 | tf_op jit(solution)/shard_map/all_gather | solution.py:31
  100.8 140.7 %reduce-scatter.4.cloned.1.call-start = ((), (), s32[]{:S(2)}) async-start(), calls=%async_computation.6 | async-start | bytes 4456448 | tf_op jit(solution)/shard_map/reduce_scatter | solution.py:93
  179.4 147.4 %reduce-scatter.8.cloned.1.call-start = ((), (), s32[]{:S(2)}) async-start(), calls=%async_computation.8 | async-start | bytes 13369344 | tf_op jit(solution)/shard_map/reduce_scatter | solution.py:101
  248.9 129.1 %reduce-scatter.6.cloned.1.call-start = ((), (), s32[]{:S(2)}) async-start(), calls=%async_computation.7 | async-start | bytes 5242880 | tf_op jit(solution)/shard_map/reduce_scatter | solution.py:98
  326.8 53.3 %collective-permute-start.3 = (f32[256,768]{0,1:T(8,128)}, f32[256,768]{0,1:T(8,128)S(1)}, u32[]{:S(2)}, u32[]{:S(2)}) collective-permute-start(f32[256,768]{0,1:T(8,128)} %reduce-scatter.8.cloned.1.call-done), channel_id=1, source_target_pairs={{64,0},{128,64},{192,128},{0,192},{65,1},{129,65},{193,129},{1,193... | collective-permute-start | bytes 2359304 | tf_op jit(solution)/shard_map/ppermute | solution.py:10
  327.9 52.2 %collective-permute-start.2 = (f32[1,256,512]{1,2,0:T(8,128)S(1)}, f32[1,256,512]{1,2,0:T(8,128)S(1)}, u32[]{:S(2)}, u32[]{:S(2)}) collective-permute-start(f32[1,256,512]{1,2,0:T(8,128)S(1)} %copy.38), channel_id=1, source_target_pairs={{192,0},{0,64},{64,128},{128,192},{193,1},{1,65},{65,129},{129,193... | collective-permute-start | bytes 1572872 | tf_op jit(solution)/shard_map/ppermute | solution.py:10
  330.5 50.7 %collective-permute-start.4 = (f32[1,256,1,256]{1,3,2,0:T(8,128)S(1)}, f32[1,256,1,256]{1,3,2,0:T(8,128)S(1)}, u32[]{:S(2)}, u32[]{:S(2)}) collective-permute-start(f32[1,256,1,256]{1,3,2,0:T(8,128)S(1)} %copy.39), channel_id=1, source_target_pairs={{192,0},{0,64},{64,128},{128,192},{193,1},{1,65},{65,129},{129,193... | collective-permute-start | bytes 786440 | tf_op jit(solution)/shard_map/ppermute | solution.py:10
  (14 other events, 896.2 us)
Sparse Core Ops, SparseCore 0:
  10.0 36.3 all-gather.5
  48.8 46.0 all-gather.3
  101.0 39.5 all-gather.7
  179.5 62.0 reduce-scatter.3
  249.0 77.7 reduce-scatter.7
  329.2 48.7 reduce-scatter.5
where the time goes:
time: 390 us; the launch traced here: 389 us
  waiting for transfers between devices  281 us (72%)
  matrix products  56.1 us (14%)
  other arithmetic  24.3 us (6%)
  between operations  14.6 us (4%)
  local copies, waits for them, and re-layouts  6.95 us (2%)
  starting transfers between devices  6.04 us (2%)
    reduce_scatter x1, waiting for transfers between devices, on_device(): lax.psum_scatter(jnp.einsum('ic,ie->ce', full, dprojected, preferred_elem...  71.1 us
    reduce_scatter x1, waiting for transfers between devices, on_device(): lax.psum_scatter(dkv_terms, 'seq', scatter_dimension=0, tiled=True)  57 us
    all_gather x1, waiting for transfers between devices, on_device(): whole_w = lax.all_gather(part_w, 'seq', axis=0, tiled=True)  48.5 us
    reduce_scatter x1, waiting for transfers between devices, on_device(): lax.psum_scatter(partial_x, 'tensor', scatter_dimension=1, tiled=True)  46.6 us
    all_gather x1, waiting for transfers between devices, on_device(): full = lax.all_gather(tokens, 'tensor', axis=2, tiled=True)[0]  26.2 us
    all_gather x1, waiting for transfers between devices, on_device(): all_kv = lax.all_gather(keyval, 'seq', axis=0, tiled=True)  22 us
    lt x1, other arithmetic, on_device(): kvalid = kpos % rows < owner  9.98 us
    dot_general x1, matrix products, on_device(): jnp.einsum('igxd,jgd->gxij', upstream_gradient, value_rows, preferred_ele...  9.53 us
  transfers between devices with their start and end apart: 11, of which 7 were waited for; matrix products, arithmetic and copies ran while one was open for 9% of the time, Pallas kernels for 0%

commit v1 on v0

v1 whole, which is shorter than its diff:
```python
import functools

import jax
import jax.numpy as jnp
from jax import lax
from jax.experimental import pallas as pl
from jax.experimental.pallas import tpu as pltpu
from jax.sharding import PartitionSpec as P

MESH = pl.DeviceIdType.MESH
BF16 = jnp.bfloat16
F32 = jnp.float32
MIB = 1 << 20
LOG2E = 1.4426950408889634
MASKED = -1e30


def matmul(a, b):
    return jnp.dot(a, b, preferred_element_type=F32)


def matmul_t(a, b):
    return lax.dot_general(a, b, (((1,), (1,)), ((), ())), preferred_element_type=F32)


class Place:
    def __init__(self, n_blk, n_seq, n_tensor):
        self.n_blk, self.chips, self.n_tensor = n_blk, n_seq // 2, n_tensor
        me = lax.axis_index("seq")
        self.core, self.chip = lax.rem(me, 2), lax.div(me, 2)
        self.blk, self.t = lax.axis_index("blk"), lax.axis_index("tensor")
        self.sibling = {"seq": me + 1 - 2 * self.core}

    def at(self, distance):
        return lax.rem(self.chip + distance + self.chips, self.chips)

    def along_seq(self, distance):
        return {"seq": 2 * self.at(distance) + self.core}

    def along_blk(self, distance):
        return {"blk": lax.rem(self.blk + distance + self.n_blk, self.n_blk)}

    def tensor_at(self, distance):
        return lax.rem(self.t + distance + self.n_tensor, self.n_tensor)

    def along_tensor(self, distance):
        return {"tensor": self.tensor_at(distance)}

    def greet(self):
        barrier = pltpu.get_barrier_semaphore()
        others = [self.sibling]
        for sign in (1, -1):
            others += [self.along_seq(sign), self.along_blk(sign), self.along_tensor(sign)]
        for other in others:
            pl.semaphore_signal(barrier, inc=1, device_id=other, device_id_type=MESH)
        pl.semaphore_wait(barrier, len(others))


class Links:
    def __init__(self, send, recv):
        self.send, self.recv, self.used, self.sent = send, recv, 0, []

    def copy(self, src, dst, to, arrives=None):
        i = self.used
        self.used += 1
        made = pltpu.make_async_remote_copy(
            src_ref=src, dst_ref=dst, send_sem=self.send.at[i], recv_sem=self.recv.at[i],
            device_id=to, device_id_type=MESH,
        )
        landing = made
        if arrives is not None:
            landing = pltpu.make_async_remote_copy(
                src_ref=arrives, dst_ref=arrives, send_sem=self.send.at[i], recv_sem=self.recv.at[i],
                device_id=to, device_id_type=MESH,
            )
        made.start()
        self.sent.append(made)
        return landing.wait_recv

    def drain(self):
        for made in self.sent:
            made.wait_send()


def gather_kernel(
    sizes, tok, wq, wkv, x2t_out, wq_out, wkv_out, kv_out, q_out,
    xb, x2t, xts, wqb, wkvb, kvb, send, recv, local,
):
    place = Place(*sizes)
    links = Links(send, recv)
    chips, half = place.chips, place.chips // 2
    rows = tok.shape[0]
    krows = wq.shape[0]
    sub = krows // 2
    halves = (pl.ds(0, sub), pl.ds(sub, sub))
    full = pl.ds(0, krows)
    c = place.core

    own_tok = pltpu.make_async_copy(tok, xb.at[place.t], local.at[0])
    own_tok.start()
    place.greet()

    def pass_on(buf, sign, step, part):
        src = buf.at[place.at(-sign * (step - 1)), c, part]
        return links.copy(src, src, place.along_seq(sign), buf.at[place.at(-sign * step), c, part])

    def both_ways(buf, step):
        parts = (full, full) if step < half else halves
        waits = [pass_on(buf, sign, step, part) for sign, part in zip((1, -1), parts)]
        return lambda: [w() for w in waits]

    def half_ways(buf, step, h):
        signs = [s for i, s in enumerate((1, -1)) if step < half or i == h]
        waits = [pass_on(buf, sign, step, halves[h]) for sign in signs]
        return lambda: [w() for w in waits]

    shared = {}

    def share(buf, key, distance):
        src = buf.at[place.at(distance), c]
        got = links.copy(src, src, place.sibling, buf.at[place.at(distance), 1 - c])
        shared.setdefault(key, []).append(got)

    def share_step(buf, key, step):
        for distance in (step, -step) if step < half else (step,):
            share(buf, key, distance)

    def collect(key):
        for got in shared[key]:
            got()

    ahead = place.along_blk(1)
    slot = place.chip
    shift_kv = links.copy(wkv, wkvb.at[slot, c], ahead)
    shift_q = [
        links.copy(wq.at[h], wqb.at[slot, c, h], ahead) for h in halves
    ]
    up = links.copy(tok, xb.at[place.t], place.along_tensor(1), xb.at[place.tensor_at(-1)])
    down = links.copy(tok, xb.at[place.t], place.along_tensor(-1), xb.at[place.tensor_at(1)])

    shift_kv()
    kv_got = both_ways(wkvb, 1)
    share(wkvb, "kv", 0)
    shift_q[0]()
    q_got = [half_ways(wqb, 1, 0), None]
    kv_got()
    kv_got = both_ways(wkvb, 2)
    share_step(wkvb, "kv", 1)
    shift_q[1]()
    q_got[1] = half_ways(wqb, 1, 1)
    share(wqb, "q", 0)

    up()
    rsub = rows // 2
    near = (pl.ds(0, rsub), pl.ds(rsub, rsub))
    src = xb.at[place.tensor_at(-1), near[0]]
    up_far = links.copy(src, src, place.along_tensor(1), xb.at[place.tensor_at(-2), near[0]])
    down()
    src = xb.at[place.tensor_at(1), near[1]]
    down_far = links.copy(src, src, place.along_tensor(-1), xb.at[place.tensor_at(2), near[1]])

    q_step = [1, 1]

    def advance_q(h):
        if q_got[h] is None:
            return
        q_got[h]()
        q_got[h] = None
        done = q_step[h]
        if done < half:
            q_step[h] += 1
            q_got[h] = half_ways(wqb, q_step[h], h)
        if h == 1 and done < half:
            share_step(wqb, "q", done)

    for step in range(2, half + 1):
        kv_got()
        if step < half:
            kv_got = both_ways(wkvb, step + 1)
        share_step(wkvb, "kv", step)
        if step < half:
            advance_q(step % 2)
    up_far()
    down_far()
    own_tok.wait()
    per = chips // sizes[2]
    collect("kv")
    keyval = None
    for t in range(sizes[2]):
        part = wkvb[t * per:(t + 1) * per].reshape(2 * per * krows, wkv.shape[1])
        term = matmul(xb[t], part)
        keyval = term if keyval is None else keyval + term
    kvb[place.chip, c] = keyval.astype(BF16)
    kv_got = both_ways(kvb, 1)
    share(kvb, "all", 0)
    save_kv = pltpu.make_async_copy(wkvb, wkv_out, local.at[1])
    save_kv.start()

    def turn(i):
        for p in range(per):
            zz = i * per + p
            mine = pl.ds(pl.multiple_of((2 * p + c) * krows, krows), krows)
            other = pl.ds(pl.multiple_of((2 * p + 1 - c) * krows, krows), krows)
            x2t[zz, :, :rows] = xb[i, :, mine].T
            xts[zz] = xb[i, :, other].T

    turns = list(range(sizes[2]))
    for step in range(1, half + 1):
        advance_q(0)
        advance_q(1)
        if turns:
            turn(turns.pop(0))
        kv_got()
        if step < half:
            kv_got = both_ways(kvb, step + 1)
        share_step(kvb, "all", step)
    while turns:
        turn(turns.pop(0))
    x_got = links.copy(
        xts, x2t.at[:, :, pl.ds(rows, rows)], place.sibling
    )
    while q_got[0] is not None or q_got[1] is not None:
        advance_q(0)
        advance_q(1)
    share(wqb, "q", half)
    collect("q")
    save_q = pltpu.make_async_copy(wqb, wq_out, local.at[2])
    save_q.start()
    query = None
    for t in range(sizes[2]):
        part = wqb[t * per:(t + 1) * per].reshape(2 * per * krows, wq.shape[1])
        term = matmul(xb[t], part)
        query = term if query is None else query + term
    q_out[...] = query.astype(BF16)
    collect("all")
    save_all = pltpu.make_async_copy(kvb, kv_out, local.at[3])
    save_all.start()
    x_got()
    save_x = pltpu.make_async_copy(x2t, x2t_out, local.at[4])
    save_x.start()
    links.drain()
    for save in (save_kv, save_q, save_all, save_x):
        save.wait()


def gather_project(sizes, tok, wq, wkv):
    n_blk, n_seq, n_tensor = sizes
    chips = n_seq // 2
    rows, krows, qcols, kcols = tok.shape[0], wq.shape[0], wq.shape[1], wkv.shape[1]
    hbm = pl.BlockSpec(memory_space=pl.ANY)
    shapes = [
        jax.ShapeDtypeStruct((chips, krows, 2 * rows), BF16),
        jax.ShapeDtypeStruct((chips, 2, krows, qcols), BF16),
        jax.ShapeDtypeStruct((chips, 2, krows, kcols), BF16),
        jax.ShapeDtypeStruct((chips, 2, rows, kcols), BF16),
        jax.ShapeDtypeStruct((rows, qcols), BF16),
    ]
    return pl.pallas_call(
        functools.partial(gather_kernel, sizes),
        out_shape=shapes,
        in_specs=[hbm] * 3,
        out_specs=[hbm] * 4 + [pl.BlockSpec(memory_space=pltpu.VMEM)],
        scratch_shapes=[
            pltpu.VMEM((n_tensor,) + tok.shape, BF16),
            pltpu.VMEM(shapes[0].shape, BF16),
            pltpu.VMEM((chips, krows, rows), BF16),
            pltpu.VMEM(shapes[1].shape, BF16),
            pltpu.VMEM(shapes[2].shape, BF16),
            pltpu.VMEM(shapes[3].shape, BF16),
            pltpu.SemaphoreType.DMA((100,)),
            pltpu.SemaphoreType.DMA((100,)),
            pltpu.SemaphoreType.DMA((5,)),
        ],
        compiler_params=pltpu.CompilerParams(
            collective_id=0, has_side_effects=True, vmem_limit_bytes=48 * MIB
        ),
        name="gather_project",
    )(tok, wq, wkv)


def attention_kernel(
    heads, me, span, counts, seg, query, kv, cot, ctx, dquery, dkv,
    s_buf, e_buf, qt, ut, o_acc, dq_acc,
):
    rows = query.shape[0]
    hs = query.shape[1] // heads
    blocks = kv.shape[0]
    total = blocks * rows
    slots = span.shape[0] // 2
    rank = me[0]
    c = hs ** -0.5 * LOG2E

    seg_all = seg[...]
    seg_q = seg[pl.ds(rank, 1), :]
    qpos = rank * rows + lax.broadcasted_iota(jnp.int32, (1, rows), 1)
    lo = jnp.zeros((1, rows), jnp.int32)
    hi = jnp.zeros((1, rows), jnp.int32)
    begin = jnp.int32(0)
    for s in range(slots):
        end = jnp.sum((seg_all <= s).astype(F32)).astype(jnp.int32)
        first, last = span[2 * s], span[2 * s + 1]
        here = seg_q == s
        inside = (qpos >= first) & (qpos < last)
        lo = jnp.where(here, begin, lo)
        hi = jnp.where(here, jnp.where(inside, jnp.minimum(last, end), qpos + 1), hi)
        begin = end
    b_lo = lax.div(jnp.min(lo.astype(F32)).astype(jnp.int32), rows)
    b_hi = lax.div(jnp.max(hi.astype(F32)).astype(jnp.int32) + rows - 1, rows)
    valid_t = lax.broadcasted_iota(jnp.int32, (1, rows), 1) < counts[rank]

    dkv[...] = jnp.zeros_like(dkv)
    o_acc[...] = jnp.zeros_like(o_acc)
    dq_acc[...] = jnp.zeros_like(dq_acc)
    for h in range(heads):
        qt[h] = query[:, h * hs:(h + 1) * hs].T
        ut[h] = jnp.where(valid_t, cot[:, h * hs:(h + 1) * hs].T.astype(F32), 0.0).astype(BF16)

    def rows8(x, op):
        return op(x.reshape(rows // 8, 8, rows), axis=0)

    def scores(b, top):
        key = kv[b, :, :hs]
        i = lax.broadcasted_iota(jnp.int32, (rows, 1), 0)
        j = jnp.where(i < counts[b], b * rows + i, -1)
        allowed = (j >= lo) & (j < hi)
        new = []
        for h in range(heads):
            s = jnp.where(allowed, matmul(key, qt[h]), MASKED)
            s_buf[b, h] = s
            new.append(jnp.maximum(top[h], rows8(s, jnp.max)))
        return tuple(new)

    start = jnp.full((8, rows), MASKED, F32)
    top = lax.fori_loop(b_lo, b_hi, scores, (start,) * heads)
    top = [jnp.max(t, axis=0, keepdims=True) * c for t in top]

    def weigh(b, total_of):
        value_t = kv[b, :, hs:].T
        new = []
        for h in range(heads):
            e = jnp.exp2(s_buf[b, h] * c - top[h])
            new.append(total_of[h] + rows8(e, jnp.sum))
            e = e.astype(BF16)
            e_buf[b, h] = e
            o_acc[h] += matmul(value_t, e)
        return tuple(new)

    totals = lax.fori_loop(b_lo, b_hi, weigh, (jnp.zeros((8, rows), F32),) * heads)
    us, deltas = [], []
    for h in range(heads):
        part = 1.0 / jnp.sum(totals[h], axis=0, keepdims=True)
        attended = jnp.where(valid_t, o_acc[h] * part, 0.0)
        ctx[:, h * hs:(h + 1) * hs] = attended.T.astype(BF16)
        u = ut[h].astype(F32) * part
        deltas.append(jnp.sum(u * attended, axis=0, keepdims=True))
        ut[h] = u.astype(BF16)
        us.append(u.T.astype(BF16))

    def back(b, carry):
        key = kv[b, :, :hs]
        value = kv[b, :, hs:]
        key_t = key.T
        dkey = dval = None
        for h in range(heads):
            e = e_buf[b, h]
            ds = (e.astype(F32) * (matmul(value, ut[h]) - deltas[h])).astype(BF16)
            dq_acc[h] += matmul(key_t, ds)
            k_term = matmul(ds, query[:, h * hs:(h + 1) * hs])
            v_term = matmul(e, us[h])
            dkey = k_term if dkey is None else dkey + k_term
            dval = v_term if dval is None else dval + v_term
        dkv[b, :, :hs] = (dkey * hs ** -0.5).astype(BF16)
        dkv[b, :, hs:] = dval.astype(BF16)
        return carry

    lax.fori_loop(b_lo, b_hi, back, 0)
    for h in range(heads):
        dquery[:, h * hs:(h + 1) * hs] = (dq_acc[h] * hs ** -0.5).T.astype(BF16)


def attention(heads, me, span, counts, seg, query, kv, cot):
    rows, qcols = query.shape
    hs = qcols // heads
    blocks = kv.shape[0]
    vmem = pl.BlockSpec(memory_space=pltpu.VMEM)
    smem = pl.BlockSpec(memory_space=pltpu.SMEM)
    return pl.pallas_call(
        functools.partial(attention_kernel, heads),
        out_shape=[
            jax.ShapeDtypeStruct((rows, qcols), BF16),
            jax.ShapeDtypeStruct((rows, qcols), BF16),
            jax.ShapeDtypeStruct(kv.shape, BF16),
        ],
        in_specs=[smem] * 3 + [vmem] * 4,
        out_specs=[vmem] * 3,
        scratch_shapes=[
            pltpu.VMEM((blocks, heads, rows, rows), F32),
            pltpu.VMEM((blocks, heads, rows, rows), BF16),
            pltpu.VMEM((heads, hs, rows), BF16),
            pltpu.VMEM((heads, hs, rows), BF16),
            pltpu.VMEM((heads, hs, rows), F32),
            pltpu.VMEM((heads, hs, rows), F32),
        ],
        compiler_params=pltpu.CompilerParams(vmem_limit_bytes=48 * MIB),
        name="attention",
    )(me, span, counts, seg, query, kv, cot)


def scatter_kernel(
    sizes, total, dkvp, dq, x2t, wq, wkv, acc_q, acc_kv, gt, out_q, out_kv,
    own, sib, dq2, dkv2, x2, wqb, wkvb, cyc_q, cyc_kv,
    kv_send, kv_recv, fq_send, fq_recv, fk_send, fk_recv, y_send, y_recv, back_q, back_kv, back_q_in, back_kv_in,
    send, recv, local,
):
    place = Place(*sizes)
    links = Links(send, recv)
    chips, half = place.chips, place.chips // 2
    n_tensor = sizes[2]
    rows, qcols = dq.shape
    krows, kcols = wkv.shape[2], wkv.shape[3]
    sub = krows // 2
    c = place.core
    halves = (slice(0, sub), slice(sub, krows))

    loads = []

    def load(src, dst):
        made = pltpu.make_async_copy(src, dst, local.at[len(loads)])
        made.start()
        loads.append(made)
        return made.wait

    have_dq = load(dq, dq2.at[pl.ds(0, rows)])
    have_own = load(dkvp.at[:, c], own)
    have_x = load(x2t, x2)
    have_wq = load(wq, wqb)
    have_wkv = load(wkv, wkvb)
    place.greet()

    distances = [half]
    for d in range(half - 1, 0, -1):
        distances += [d, -d]
    distances.append(0)
    from_sibling = {}
    for d in distances[:1]:
        from_sibling[d] = links.copy(dkvp.at[place.at(d), 1 - c], sib.at[place.at(d)], place.sibling)
    sib_dq = links.copy(dq, dq2.at[pl.ds(rows, rows)], place.sibling)
    for d in distances[1:]:
        from_sibling[d] = links.copy(dkvp.at[place.at(d), 1 - c], sib.at[place.at(d)], place.sibling)
    from_sibling[-half] = lambda: None
    got_cyc_q = links.copy(acc_q, cyc_q, place.along_blk(1))
    got_cyc_kv = links.copy(acc_kv, cyc_kv, place.along_blk(1))

    class Ring:
        def __init__(self, term, sign, n, out, came, first=None):
            self.term, self.sign, self.n, self.out, self.came = term, sign, n, out, came
            self.first, self.k, self.wait = first, 0, None

        def part(self, k):
            return self.first if k == 1 and self.first is not None else slice(0, self.out.shape[1])

        def ref(self, buf, k):
            part = self.part(k)
            return buf.at[k - 1, pl.ds(part.start, part.stop - part.start)]

        def step(self):
            if self.k == self.n:
                return
            self.k = k = self.k + 1
            part = self.part(k)
            value = self.term(self.sign * (self.n - k + 1), part)
            if k == 1:
                self.out[0, part] = value.astype(BF16)
            else:
                before = self.part(k - 1)
                self.wait()
                came = self.came[k - 2, before].astype(F32)
                if before == part:
                    self.out[k - 1] = (value + came).astype(BF16)
                else:
                    other = halves[1] if before == halves[0] else halves[0]
                    self.out[k - 1, before] = (value[before] + came).astype(BF16)
                    self.out[k - 1, other] = value[other].astype(BF16)
            self.wait = links.copy(
                self.ref(self.out, k), self.ref(self.came, k), place.along_seq(self.sign)
            )

        def result(self):
            self.wait()
            return self.came[self.n - 1].astype(F32)

    def kv_term(d, part):
        if part.start == 0 or d != half and d != -half:
            from_sibling[d]()
        here = place.at(d)
        return own[here, part].astype(F32) + sib[here, part].astype(F32)

    def q_term(offset):
        return lambda d, part: matmul(x2[place.at(d), offset:offset + sub], dq2[...])

    def k_term(d, part):
        return matmul(x2[place.at(d), part], dkv2[...])

    kv_rings = [
        Ring(kv_term, sign, half, kv_send.at[i], kv_recv.at[i], halves[i]) for i, sign in enumerate((1, -1))
    ]
    q_rings = []
    for h in range(2):
        for i, sign in enumerate((1, -1)):
            n = half if h == i else half - 1
            q_rings.append(
                Ring(q_term(h * sub), sign, n, fq_send.at[2 * h + i], fq_recv.at[2 * h + i])
            )
    k_rings = [
        Ring(k_term, sign, half, fk_send.at[i], fk_recv.at[i], halves[i]) for i, sign in enumerate((1, -1))
    ]

    def step(rings):
        for ring in rings:
            ring.step()

    long_q = [q_rings[0], q_rings[3]]
    short_q = [q_rings[2], q_rings[1]]

    have_own()
    step(kv_rings)
    have_dq()
    have_x()
    sib_dq()
    step(long_q)
    step(kv_rings)
    step(short_q)
    step(kv_rings)
    step(long_q)
    step(kv_rings)
    step(short_q)
    from_sibling[0]()
    dkeyval = own[place.chip].astype(F32) + sib[place.chip].astype(F32)
    step(long_q)
    dkeyval += kv_rings[0].result() + kv_rings[1].result()
    dkv2[:rows] = dkeyval.astype(BF16)
    sib_dkv = links.copy(dkv2.at[pl.ds(0, rows)], dkv2.at[pl.ds(rows, rows)], place.sibling)

    have_wq()
    have_wkv()
    per = chips // n_tensor

    def grad_term(distance, part):
        t = place.tensor_at(distance)
        shard = 2 * per * krows
        w_q = wqb[pl.ds(t * per, per)].reshape(shard, qcols)
        w_kv = wkvb[pl.ds(t * per, per)].reshape(shard, kcols)
        return matmul_t(dq2[part], w_q) + matmul_t(dkv2[part], w_kv)

    rsub = rows // 2
    rhalves = (slice(0, rsub), slice(rsub, rows))
    y_far = []
    far = grad_term(2, slice(0, rows))
    for i, sign in enumerate((1, -1)):
        y_send[i, 0, rhalves[i]] = far[rhalves[i]].astype(BF16)
        ref = pl.ds(rhalves[i].start, rsub)
        y_far.append(links.copy(y_send.at[i, 0, ref], y_recv.at[i, 0, ref], place.along_tensor(sign)))
    sib_dkv()
    step(k_rings)
    step(short_q)
    step(k_rings)
    y_near = []
    for i, sign in enumerate((1, -1)):
        near = grad_term(sign, slice(0, rows))
        y_far[i]()
        mine, other = rhalves[i], rhalves[1 - i]
        y_send[i, 1, mine] = (near[mine] + y_recv[i, 0, mine].astype(F32)).astype(BF16)
        y_send[i, 1, other] = near[other].astype(BF16)
        y_near.append(links.copy(y_send.at[i, 1], y_recv.at[i, 1], place.along_tensor(sign)))
    step(long_q)
    step(k_rings)
    fresh = []
    for h in range(2):
        mine = matmul(x2[place.chip, halves[h]], dq2[...])
        fresh.append(mine + q_rings[2 * h].result() + q_rings[2 * h + 1].result())
    step(k_rings)
    got_back_q = []
    for h in range(2):
        back_q[halves[h]] = (fresh[h] / total).astype(BF16)
        ref = pl.ds(halves[h].start, sub)
        got_back_q.append(links.copy(back_q.at[ref], back_q_in.at[ref], place.along_blk(-1)))
    home = grad_term(0, slice(0, rows))
    for wait in y_near:
        wait()
    gt[...] = (home + y_recv[0, 1].astype(F32) + y_recv[1, 1].astype(F32)).astype(BF16)
    fresh_kv = matmul(x2[place.chip], dkv2[...]) + k_rings[0].result() + k_rings[1].result()
    back_kv[...] = (fresh_kv / total).astype(BF16)
    got_back_kv = links.copy(back_kv, back_kv_in, place.along_blk(-1))
    got_cyc_q()
    got_cyc_kv()
    for got in got_back_q:
        got()
    out_q[...] = cyc_q[...] + back_q_in[...].astype(F32)
    got_back_kv()
    out_kv[...] = cyc_kv[...] + back_kv_in[...].astype(F32)
    links.drain()


def scatter_grads(sizes, total, dkvp, dq, x2t, wq, wkv, acc_q, acc_kv, width):
    n_blk, n_seq, n_tensor = sizes
    chips = n_seq // 2
    half = chips // 2
    rows, qcols = dq.shape
    krows, kcols = wkv.shape[2], wkv.shape[3]
    sub = krows // 2
    hbm = pl.BlockSpec(memory_space=pl.ANY)
    vmem = pl.BlockSpec(memory_space=pltpu.VMEM)
    return pl.pallas_call(
        functools.partial(scatter_kernel, sizes, total),
        out_shape=[
            jax.ShapeDtypeStruct((rows, width), BF16),
            jax.ShapeDtypeStruct((krows, qcols), F32),
            jax.ShapeDtypeStruct((krows, kcols), F32),
        ],
        in_specs=[hbm] * 7,
        out_specs=[vmem] * 3,
        scratch_shapes=[
            pltpu.VMEM((chips, rows, kcols), BF16),
            pltpu.VMEM((chips, rows, kcols), BF16),
            pltpu.VMEM((2 * rows, qcols), BF16),
            pltpu.VMEM((2 * rows, kcols), BF16),
            pltpu.VMEM(x2t.shape, BF16),
            pltpu.VMEM(wq.shape, BF16),
            pltpu.VMEM(wkv.shape, BF16),
            pltpu.VMEM((krows, qcols), F32),
            pltpu.VMEM((krows, kcols), F32),
            pltpu.VMEM((2, half, rows, kcols), BF16),
            pltpu.VMEM((2, half, rows, kcols), BF16),
            pltpu.VMEM((4, half, sub, qcols), BF16),
            pltpu.VMEM((4, half, sub, qcols), BF16),
            pltpu.VMEM((2, half, krows, kcols), BF16),
            pltpu.VMEM((2, half, krows, kcols), BF16),
            pltpu.VMEM((2, 2, rows, width), BF16),
            pltpu.VMEM((2, 2, rows, width), BF16),
            pltpu.VMEM((krows, qcols), BF16),
            pltpu.VMEM((krows, kcols), BF16),
            pltpu.VMEM((krows, qcols), BF16),
            pltpu.VMEM((krows, kcols), BF16),
            pltpu.SemaphoreType.DMA((64,)),
            pltpu.SemaphoreType.DMA((64,)),
            pltpu.SemaphoreType.DMA((5,)),
        ],
        compiler_params=pltpu.CompilerParams(
            collective_id=1, has_side_effects=True, vmem_limit_bytes=56 * MIB
        ),
        name="scatter_grads",
    )(dkvp, dq, x2t, wq, wkv, acc_q, acc_kv)


def on_device(
    sizes, tokens, w_query, w_keyval, accum_query, accum_keyval, cotangent, seg_ids, spans, counts
):
    n_seq = sizes[1]
    rows, width = tokens.shape[1:]
    krows, qcols = w_query.shape[1:]
    groups, kv_cols = w_keyval.shape[2:]
    kcols = groups * kv_cols
    heads = qcols // (kv_cols // 2)
    total = rows * n_seq
    x2t, wq_all, wkv_all, kv_all, query = gather_project(
        sizes, tokens[0], w_query[0], w_keyval[0].reshape(krows, kcols)
    )
    me = lax.axis_index("seq").astype(jnp.int32).reshape(1)
    context, dquery, dkv = attention(
        heads, me, spans[0].reshape(-1), counts[0], seg_ids[0].reshape(n_seq, rows),
        query, kv_all.reshape(n_seq, rows, kcols), cotangent[0],
    )
    grad_tokens, out_q, out_kv = scatter_grads(
        sizes, total, dkv.reshape(kv_all.shape), dquery, x2t, wq_all, wkv_all,
        accum_query[0], accum_keyval[0].reshape(krows, kcols), width,
    )
    return context[None], grad_tokens[None], out_q[None], out_kv.reshape(w_keyval.shape)


def solution(mesh):
    sizes = (mesh.shape["blk"], mesh.shape["seq"], mesh.shape["tensor"])
    in_specs = (
        P("blk", "seq", "tensor"),
        P("blk", "seq", "tensor"),
        P("blk", "seq", "tensor", None),
        P("blk", "seq", "tensor"),
        P("blk", "seq", "tensor", None),
        P("blk", "seq", "tensor"),
        P("blk", None),
        P("blk", None, None),
        P("blk", None),
    )
    out_specs = (
        P("blk", "seq", "tensor"),
        P("blk", "seq", "tensor"),
        P("blk", "seq", "tensor"),
        P("blk", "seq", "tensor", None),
    )
    return jax.shard_map(
        functools.partial(on_device, sizes), mesh=mesh, in_specs=in_specs, out_specs=out_specs, check_vma=False
    )
```

time: 390 us -> 164 us (0.42)
  waiting for transfers between devices: 281 us -> 0 us
  Pallas kernels: 0 us -> 142 us
  matrix products: 56.1 us -> 0 us
  other arithmetic: 24.3 us -> 1.4 us
  between operations: 14.6 us -> 0.69 us
  local copies, waits for them, and re-layouts: 6.95 us -> 18.6 us
  starting transfers between devices: 6.04 us -> 0 us
    reduce_scatter x3 -> x0, waiting for transfers between devices: 175 us -> none  [the longest x1 71.1 us: on_device(): lax.psum_scatter(jnp.einsum('ic,ie->ce', full, dprojected, preferred_elem...]
    pallas_call x0 -> x3, Pallas kernels: none -> 142 us  [the longest x1 71.7 us: scatter_grads(): pl.pallas_call(functools.partial(scatter_kernel, sizes, total), out_shape...]
    all_gather x3 -> x0, waiting for transfers between devices: 96.7 us -> none  [the longest x1 48.5 us: on_device(): whole_w = lax.all_gather(part_w, 'seq', axis=0, tiled=True)]
    dot_general x9 -> x0, matrix products: 56.1 us -> none  [the longest x1 9.53 us: on_device(): jnp.einsum('igxd,jgd->gxij', upstream_gradient, value_rows, preferred_ele...]
    unnamed x60 -> x28, local copies, waits for them, and re-layouts: 4.01 us -> 18.5 us
    lt x1 -> x0, other arithmetic: 9.98 us -> none  [on_device(): kvalid = kpos % rows < owner]
    ppermute x5 -> x0, waiting for transfers between devices: 8.77 us -> none  [passed_along(): return lax.ppermute(block, axis, route)]
    ppermute x5 -> x0, starting transfers between devices: 5.79 us -> none  [passed_along(): return lax.ppermute(block, axis, route)]
  transfers between devices with their start and end apart: 11 -> 0, of which waited for: 7 -> 0; matrix products, arithmetic and copies ran while one was open for 9% -> 0% of each run, Pallas kernels for 0% -> 0%
where the time goes in v1:
time: 164 us; the launch traced here: 163 us
  Pallas kernels  142 us (87%)
  local copies, waits for them, and re-layouts  18.6 us (11%)
    pallas_call x1, Pallas kernels, scatter_grads(): pl.pallas_call(functools.partial(scatter_kernel, sizes, total), out_shape...  71.7 us
    pallas_call x1, Pallas kernels, gather_project(): pl.pallas_call(functools.partial(gather_kernel, sizes), out_shape=shapes,...  66.2 us
    unnamed x28, local copies, waits for them, and re-layouts  18.5 us
    pallas_call x1, Pallas kernels, attention(): pl.pallas_call(functools.partial(attention_kernel, heads), out_shape=[jax...  4.01 us

profile of v1, /device:TPU:6, one launch (start us, length us, event | category | flops | bytes accessed | tf_op | source)
XLA Modules:
  0.0 162.6 jit_solution(16818340338445914598)
XLA Ops:
  0.6 0.0 copy-start.4
  0.6 1.0 copy-done.4
  1.7 0.9 copy-done.5
  2.6 0.9 copy-done.8
  3.5 66.2 %gather_project.1 = (bf16[8,256,512]{2,1,0:T(8,128)(2,1)S(1)}, bf16[8,2,256,512]{3,2,1,0:T(8,128)(2,1)}, bf16[8,2,256,256]{3,2,1,0:T(8,128)(2,1)S(1)}, bf16[8,2,...) custom-call(bf16[256,1024]{1,0:T(8,128)(2,1)S(1)} %bitcast.18, bf16[256,512]{1,0:T(8,128)(2,1)S(1)} %bitcast.19, ...), custom_call_target="tpu_custom_call" | custom-call | tf_op jit(solution)/shard_map/gather_project/pallas_call | solution.py:258
  69.8 0.0 copy-start.1
  69.8 1.3 copy-done.1
  71.1 1.3 copy-done.2
  72.4 0.5 broadcast.3
  73.0 1.4 reduce.3
  74.4 0.8 copy.15
  75.1 0.1 reshape_squeeze.12.span
  75.2 1.6 copy-done
  76.8 0.9 copy-done.7
  77.8 0.7 copy-done.9
  78.4 4.0 %attention.1 = (bf16[256,512]{1,0:T(8,128)(2,1)}, bf16[256,512]{1,0:T(8,128)(2,1)S(1)}, bf16[16,256,256]{2,1,0:T(8,128)(2,1)S(1)}) custom-call(s32[1]{0:T(128)} %bitcast.me, s32[16]{0:T(128)S(1)} %reshape_squeeze.12.span, s32[16]{0:T(128)S(1)} %bitcast.22, s32[16,256]{1,0:T(8,128)S(1)} %reshape_squeeze.13.seg, bf16[256,512]{1,0:T(8,128)(2,1)S(1)} %get-tuple-element.15.query, ...), custom_call_target="tpu_custom_call" | custom-call | tf_op jit(solution)/shard_map/attention/pallas_call | solution.py:387
  82.4 1.4 copy-done.3
  83.8 0.7 copy-done.6
  84.5 0.0 copy-done.10
  84.5 0.7 copy.19
  85.2 71.7 %scatter_grads.1 = (bf16[256,1024]{1,0:T(8,128)(2,1)}, f32[256,512]{1,0:T(8,128)}, f32[256,256]{1,0:T(8,128)}) custom-call(bf16[8,2,256,256]{3,2,1,0:T(8,128)(2,1)} %bitcast.17, bf16[256,512]{1,0:T(8,128)(2,1)} %copy-done.6, bf16[8,256,512]{2,1,0:T(8,128)(2,1)} %copy-done.1, bf16[8,2,256,512]{3,2,1,0:T(8,128)(2,1)} %get-tuple-element.21.wq, ...), custom_call_target="tpu_custom_call" | custom-call | tf_op jit(solution)/shard_map/scatter_grads/pallas_call | solution.py:613
  156.9 1.9 %copy.16 = f32[1,256,1,256]{3,2,1,0:T(1,128)} copy(f32[1,256,1,256]{3,1,2,0:T(8,128)} %bitcast.27) | data formatting | bytes 524288
  158.8 1.9 %copy.22 = bf16[1,256,1024]{2,1,0:T(8,128)(2,1)} copy(bf16[1,256,1024]{2,1,0:T(8,128)(2,1)} %bitcast.26) | data formatting | bytes 1048576
  160.7 1.9 %copy.23 = f32[1,256,512]{2,1,0:T(8,128)} copy(f32[1,256,512]{2,1,0:T(8,128)} %bitcast.25) | data formatting | bytes 1048576
  (10 shorter events, 0.0 us)
Async XLA Ops:
  0.6 1.0 copy-start.4
  1.7 0.9 copy-start.5
  2.6 0.9 copy-start.8
  3.5 81.0 %copy-start.10 = (f32[1,256,1,256]{3,2,1,0:T(1,128)S(1)}, f32[1,256,1,256]{3,2,1,0:T(1,128)}, u32[]{:S(2)}) copy-start(f32[1,256,1,256]{3,2,1,0:T(1,128)} %param.13) | copy-start | bytes 786436
  69.8 1.3 copy-start.1
  71.1 1.3 copy-start.2
  75.2 1.6 copy-start
  76.8 0.9 copy-start.7
  77.8 0.7 copy-start.9
  82.4 1.4 copy-start.3
  83.8 0.7 copy-start.6

commit v2 on v0

v2 whole, which is shorter than its diff:
```python
import functools

import jax
import jax.numpy as jnp
from jax import lax
from jax.experimental import pallas as pl
from jax.experimental.pallas import tpu as pltpu
from jax.sharding import PartitionSpec as P

MESH = pl.DeviceIdType.MESH
BF16 = jnp.bfloat16
F32 = jnp.float32
MIB = 1 << 20
LOG2E = 1.4426950408889634
MASKED = -1e30
PAIR = 2
FILLS = (0, 1, 2, 0, 2, 1, 0, 2, 0, 2, 1, 0, 0, 1, 2, 1, 1, 0, 2, 5, 0, 1, 1, 1, 1, 2, 2, 1, 2, 2, 1, 0, 0, 1, 2)


def matmul(a, b):
    return jnp.dot(a, b, preferred_element_type=F32)


def matmul_t(a, b):
    return lax.dot_general(a, b, (((1,), (1,)), ((), ())), preferred_element_type=F32)


class Place:
    def __init__(self, n_blk, n_seq, n_tensor):
        self.n_blk, self.chips, self.n_tensor = n_blk, n_seq // 2, n_tensor
        me = lax.axis_index("seq")
        self.core, self.chip = lax.rem(me, 2), lax.div(me, 2)
        self.blk, self.t = lax.axis_index("blk"), lax.axis_index("tensor")
        self.sibling = {"seq": me + 1 - 2 * self.core}

    def at(self, distance):
        return lax.rem(self.chip + distance + self.chips, self.chips)

    def along_seq(self, distance):
        return {"seq": 2 * self.at(distance) + self.core}

    def along_blk(self, distance):
        return {"blk": lax.rem(self.blk + distance + self.n_blk, self.n_blk)}

    def tensor_at(self, distance):
        return lax.rem(self.t + distance + self.n_tensor, self.n_tensor)

    def along_tensor(self, distance):
        return {"tensor": self.tensor_at(distance)}

    def greet(self):
        barrier = pltpu.get_barrier_semaphore()
        others = [self.sibling]
        for sign in (1, -1):
            others += [self.along_seq(sign), self.along_blk(sign), self.along_tensor(sign)]
        for other in others:
            pl.semaphore_signal(barrier, inc=1, device_id=other, device_id_type=MESH)
        pl.semaphore_wait(barrier, len(others))


class Links:
    def __init__(self, send, recv):
        self.send, self.recv, self.used, self.sent = send, recv, 0, []

    def copy(self, src, dst, to, arrives=None):
        i = self.used
        self.used += 1
        made = pltpu.make_async_remote_copy(
            src_ref=src, dst_ref=dst, send_sem=self.send.at[i], recv_sem=self.recv.at[i],
            device_id=to, device_id_type=MESH,
        )
        landing = made
        if arrives is not None:
            landing = pltpu.make_async_remote_copy(
                src_ref=arrives, dst_ref=arrives, send_sem=self.send.at[i], recv_sem=self.recv.at[i],
                device_id=to, device_id_type=MESH,
            )
        made.start()
        self.sent.append(made)
        return landing.wait_recv

    def drain(self):
        for made in self.sent:
            made.wait_send()


class Gather:
    def __init__(self, place, links, buf):
        self.place, self.links, self.buf = place, links, buf
        self.half = place.chips // 2
        sub = buf.shape[2] // 2
        self.parts = (pl.ds(0, sub), pl.ds(sub, sub))
        self.done, self.waits, self.shares, self.finished = [0, 0], [None, None], [], False

    def start(self, h):
        place, c = self.place, self.place.core
        self.done[h] = step = self.done[h] + 1
        self.waits[h] = []
        for i, sign in enumerate((1, -1)):
            if step == self.half and i != h:
                continue
            src = self.buf.at[place.at(-sign * (step - 1)), c, self.parts[h]]
            lands = self.buf.at[place.at(-sign * step), c, self.parts[h]]
            self.waits[h].append(self.links.copy(src, src, place.along_seq(sign), lands))

    def share(self, distance):
        place = self.place
        src = self.buf.at[place.at(distance), place.core]
        lands = self.buf.at[place.at(distance), 1 - place.core]
        self.shares.append(self.links.copy(src, src, place.sibling, lands))

    def advance(self, h):
        step = self.done[h]
        for wait in self.waits[h]:
            wait()
        if step < self.half:
            self.start(h)
        if h == 1:
            self.finished = step == self.half
            for distance in (step, -step) if step < self.half else (step,):
                self.share(distance)

    def collect(self):
        for wait in self.shares:
            wait()


class Scatter:
    def __init__(self, place, links, term, out, came):
        self.place, self.links, self.term, self.out, self.came = place, links, term, out, came
        self.half = place.chips // 2
        self.sub = out.shape[2]
        self.done, self.waits = [0, 0], [[None, None], [None, None]]

    def rows(self, h):
        return slice(h * self.sub, (h + 1) * self.sub)

    def reach(self, h, i):
        return self.half if h == i else self.half - 1

    def step(self, h):
        self.done[h] = k = self.done[h] + 1
        for i, sign in enumerate((1, -1)):
            n = self.reach(h, i)
            if k > n:
                continue
            at = 2 * h + i
            value = self.term(sign * (n - k + 1), self.rows(h))
            if k > 1:
                self.waits[h][i]()
                value += self.came[at, k - 2].astype(F32)
            self.out[at, k - 1] = value.astype(BF16)
            self.waits[h][i] = self.links.copy(
                self.out.at[at, k - 1], self.came.at[at, k - 1], self.place.along_seq(sign)
            )

    def result(self, h):
        value = self.term(0, self.rows(h))
        for i in range(2):
            self.waits[h][i]()
            value += self.came[2 * h + i, self.reach(h, i) - 1].astype(F32)
        return value


def layer_kernel(
    sizes, heads, pair, total, tok, wq, wkv, cot, acc_q, acc_kv, seg, span, counts,
    ctx_out, gt_out, out_q_out, out_kv_out,
    ctx, gt, out_q, out_kv, xb, x2t, xts, wqbs, wkvb, kvb, cotb, qb, qt, ut, bias, s_buf, e_buf, o_acc, dq_acc, dk_acc, dkvb, sib,
    dq2, dkv2, rq_send, rq_recv, r_send, r_recv, y_send, y_recv, back_q, back_q_in, back_kv, back_kv_in,
    cyc_q, cyc_kv, send, recv, local,
):
    place = Place(*sizes)
    links = Links(send, recv)
    n_tensor = sizes[2]
    chips, half = place.chips, place.chips // 2
    per = chips // n_tensor
    rows = tok.shape[0]
    krows, kcols = wkv.shape
    hs = kcols // 2
    groups = heads // pair
    pcols = pair * hs
    c = place.core
    sub, rsub = krows // 2, rows // 2
    wqb = [wqbs.at[g] for g in range(groups)]

    own_tok = pltpu.make_async_copy(tok, xb.at[place.t], local.at[0])
    own_tok.start()
    own_cot = pltpu.make_async_copy(cot, cotb, local.at[1])
    own_cot.start()
    place.greet()

    ahead = place.along_blk(1)
    halves = (pl.ds(0, sub), pl.ds(sub, sub))
    shift_kv = [links.copy(wkv.at[h], wkvb.at[place.chip, c, h], ahead) for h in halves]
    rhalves = (pl.ds(0, rsub), pl.ds(rsub, rsub))
    near = [[None, None], [None, None]]
    for first in range(2):
        for i, sign in enumerate((1, -1)):
            h = i if first == 0 else 1 - i
            near[i][h] = links.copy(
                tok.at[rhalves[h]], xb.at[place.t, rhalves[h]], place.along_tensor(sign),
                xb.at[place.tensor_at(-sign), rhalves[h]],
            )
    shift_q = [
        links.copy(wq.at[:, pl.ds(p * pcols, pcols)], wqb[p].at[place.chip, c], ahead)
        for p in range(groups)
    ]

    g_wkv = Gather(place, links, wkvb)
    g_wq = [Gather(place, links, buf) for buf in wqb]
    g_kv = Gather(place, links, kvb)

    later = []

    counts_of = iter(FILLS)

    def fill(n=None):
        for _ in range(next(counts_of) if n is None else n):
            if later:
                later.pop(0)()

    def both(ring, move="advance"):
        for h in range(2):
            getattr(ring, move)(h)

    def first_share(p):
        shift_q[p]()
        g_wq[p].share(0)
        g_wq[p].start(0)

    for p in range(groups):
        later.append(functools.partial(first_share, p))
        later.append(functools.partial(g_wq[p].start, 1))
        for _ in range(half):
            later.append(functools.partial(g_wq[p].advance, 0))
            later.append(functools.partial(g_wq[p].advance, 1))

    for h in range(2):
        shift_kv[h]()
        g_wkv.start(h)
    g_wkv.share(0)
    both(g_wkv)
    fill()
    far = []
    for i, sign in enumerate((1, -1)):
        near[i][i]()
        src = xb.at[place.tensor_at(-sign), rhalves[i]]
        far.append(links.copy(
            src, src, place.along_tensor(sign), xb.at[place.tensor_at(-2 * sign), rhalves[i]]
        ))
    fill()

    me = 2 * place.chip + c
    slots = span.shape[1]
    seg_all = seg[...]
    seg_q = seg[:, pl.ds(pl.multiple_of(me * rows, rows), rows)]
    lane = lax.broadcasted_iota(jnp.int32, (1, rows), 1)
    qpos = me * rows + lane
    lo = jnp.zeros((1, rows), jnp.int32)
    hi = jnp.zeros((1, rows), jnp.int32)
    begin = jnp.zeros((1, 1), jnp.int32)
    for s in range(slots):
        end = jnp.sum((seg_all <= s).astype(F32), axis=1, keepdims=True).astype(jnp.int32)
        first, last = span[0, s, 0], span[0, s, 1]
        here = seg_q == s
        inside = (qpos >= first) & (qpos < last)
        lo = jnp.where(here, begin, lo)
        hi = jnp.where(here, jnp.where(inside, jnp.minimum(last, end), qpos + 1), hi)
        begin = end
    valid_t = lane < counts[0, me]
    row = lax.broadcasted_iota(jnp.int32, (rows, 1), 0)

    def mask(blocks):
        for b in blocks:
            j = jnp.where(row < counts[0, b], b * rows + row, -1)
            bias[b] = jnp.where((j >= lo) & (j < hi), 0.0, MASKED)

    mask(range(chips))
    both(g_wkv)
    fill()
    mask(range(chips, 2 * chips))
    both(g_wkv)
    fill()
    own_cot.wait()
    for h in range(heads):
        u = cotb[:, h * hs:(h + 1) * hs].T
        ut[h] = jnp.where(valid_t, u.astype(F32), 0.0).astype(BF16)
    fill()
    both(g_wkv)
    fill()
    for i in range(2):
        near[i][1 - i]()
        far[i]()
    own_tok.wait()
    g_wkv.collect()

    def project(buf):
        out = None
        for t in range(n_tensor):
            part = buf[t * per:(t + 1) * per].reshape(2 * per * krows, buf.shape[3])
            term = matmul(xb[t], part)
            out = term if out is None else out + term
        return out.astype(BF16)

    kvb[place.chip, c] = project(wkvb)
    both(g_kv, "start")
    g_kv.share(0)
    fill()
    saves = []

    def save(src, dst):
        saves.append(pltpu.make_async_copy(src, dst, local.at[2 + len(saves)]))
        saves[-1].start()

    got_cyc = [links.copy(acc_q, cyc_q, ahead), links.copy(acc_kv, cyc_kv, ahead)]

    x_got = []

    def turn(t):
        for p in range(per):
            z = t * per + p
            mine = pl.ds(pl.multiple_of((2 * p + c) * krows, krows), krows)
            other = pl.ds(pl.multiple_of((2 * p + 1 - c) * krows, krows), krows)
            x2t[z, :, :rows] = xb[t, :, mine].T
            xts[z] = xb[t, :, other].T
        z = pl.ds(t * per, per)
        x_got.append(links.copy(xts.at[z], x2t.at[z, :, pl.ds(rows, rows)], place.sibling))

    def queries(p):
        while not g_wq[p].finished:
            fill(1)
        g_wq[p].collect()
        qb[p] = project(wqb[p])
        for i in range(pair):
            qt[pair * p + i] = qb[p, :, i * hs:(i + 1) * hs].T

    turns = list(range(n_tensor))
    for step in range(half):
        for _ in range(2 if step == 1 else 1):
            if turns:
                turn(turns.pop(0))
        if step == half - 1:
            queries(0)
        fill()
        both(g_kv)
        fill()
    while turns:
        turn(turns.pop(0))
    g_kv.collect()

    def rows8(x, op):
        return op(x.reshape(x.shape[0] // 8, 8, rows), axis=0)

    scale = hs ** -0.5
    n_keys = chips * rows

    def attend(p):
        last = p == groups - 1

        def tick(enough=False):
            if not enough:
                fill()

        tops = [jnp.full((8, rows), MASKED, F32)] * pair
        for part in range(2):
            z = slice(part * half, (part + 1) * half)
            b = slice(part * chips, (part + 1) * chips)
            for i in range(pair):
                key = kvb[z, :, :, :hs].reshape(n_keys, hs)
                s = matmul(key, qt[pair * p + i]) + bias[b].reshape(n_keys, rows)
                s_buf[i, part] = s
                tops[i] = jnp.maximum(tops[i], rows8(s, jnp.max))
            tick()
        tops = [jnp.max(t, axis=0, keepdims=True) * (scale * LOG2E) for t in tops]
        sums = [jnp.zeros((8, rows), F32)] * pair
        for part in range(2):
            z = slice(part * half, (part + 1) * half)
            for i in range(pair):
                e = jnp.exp2(s_buf[i, part] * (scale * LOG2E) - tops[i])
                sums[i] = sums[i] + rows8(e, jnp.sum)
                e = e.astype(BF16)
                e_buf[i, part] = e
                term = matmul(kvb[z, :, :, hs:].reshape(n_keys, hs).T, e)
                o_acc[i] = term if part == 0 else o_acc[i] + term
            tick()
        us, deltas = [], []
        for i in range(pair):
            h = pair * p + i
            inverse = 1.0 / jnp.sum(sums[i], axis=0, keepdims=True)
            attended = jnp.where(valid_t, o_acc[i] * inverse, 0.0)
            ctx[:, h * hs:(h + 1) * hs] = attended.T.astype(BF16)
            u = ut[h].astype(F32) * inverse
            deltas.append(jnp.sum(u * attended, axis=0, keepdims=True))
            ut[h] = u.astype(BF16)
            us.append(u.T.astype(BF16))
        for part in range(2):
            z = slice(part * half, (part + 1) * half)
            dkey = dval = None
            for i in range(pair):
                h = pair * p + i
                e = e_buf[i, part]
                dp = matmul(kvb[z, :, :, hs:].reshape(n_keys, hs), ut[h])
                ds = (e.astype(F32) * (dp - deltas[i])).astype(BF16)
                term = matmul(kvb[z, :, :, :hs].reshape(n_keys, hs).T, ds)
                dq_acc[i] = term if part == 0 else dq_acc[i] + term
                k_term = matmul(ds, qb[p, :, i * hs:(i + 1) * hs])
                v_term = matmul(e, us[i])
                dkey = k_term if dkey is None else dkey + k_term
                dval = v_term if dval is None else dval + v_term
            if p > 0:
                dkey += dk_acc[part, :, :hs]
                dval += dk_acc[part, :, hs:]
            if last:
                dkvb[z, :, :, :hs] = (dkey * scale).astype(BF16).reshape(half, 2, rows, hs)
                dkvb[z, :, :, hs:] = dval.astype(BF16).reshape(half, 2, rows, hs)
                zz = pl.ds(part * half, half)
                exchanged.append(links.copy(dkvb.at[zz, 1 - c], sib.at[zz], place.sibling))
            else:
                dk_acc[part, :, :hs] = dkey
                dk_acc[part, :, hs:] = dval
            tick(part == 1)
        for i in range(pair):
            dq2[p, :rows, i * hs:(i + 1) * hs] = (dq_acc[i] * scale).T.astype(BF16)
        mine = dq2.at[p, pl.ds(0, rows)]
        got_dq = links.copy(mine, dq2.at[p, pl.ds(rows, rows)], place.sibling)

        def first_step():
            got_dq()
            s_q[p].step(0)

        later.append(first_step)
        later.append(functools.partial(s_q[p].step, 1))
        for _ in range(half - 1):
            later.append(functools.partial(s_q[p].step, 0))
            later.append(functools.partial(s_q[p].step, 1))
        later.append(functools.partial(hand_back, s_q[p], back_q.at[p], back_q_in.at[p], 0))
        later.append(functools.partial(hand_back, s_q[p], back_q.at[p], back_q_in.at[p], 1))

    exchanged = []

    def fresh_term(grads):
        return lambda d, part: matmul(x2t[place.at(d), part], grads[...])

    def kv_term(d, part):
        here = place.at(d)
        return dkvb[here, c, part].astype(F32) + sib[here, part].astype(F32)

    s_q = [
        Scatter(place, links, fresh_term(dq2.at[p]), rq_send.at[p], rq_recv.at[p]) for p in range(groups)
    ]
    s_kv = Scatter(place, links, kv_term, r_send.at[0], r_recv.at[0])
    s_k = Scatter(place, links, fresh_term(dkv2), r_send.at[1], r_recv.at[1])
    got_back = []

    def hand_back(scatter, out, came, h):
        part = pl.ds(h * sub, sub)
        out[part] = (scatter.result(h) / total).astype(BF16)
        got_back.append(links.copy(out.at[part], came.at[part], place.along_blk(-1)))

    attend(0)
    for wait in x_got:
        wait()
    for p in range(1, groups):
        queries(p)
        fill()
        attend(p)
    save(ctx, ctx_out)
    for wait in exchanged:
        wait()
    for _ in range(half):
        both(s_kv, "step")
        fill()
    for h in range(2):
        dkv2[h * rsub:(h + 1) * rsub] = s_kv.result(h).astype(BF16)
    got_dkv = links.copy(dkv2.at[pl.ds(0, rows)], dkv2.at[pl.ds(rows, rows)], place.sibling)

    shard = 2 * per * krows

    def grad_term(distance, part):
        t = place.tensor_at(distance)
        value = matmul_t(dkv2[part], wkvb[pl.ds(t * per, per)].reshape(shard, kcols))
        for p in range(groups):
            value += matmul_t(dq2[p, part], wqb[p][pl.ds(t * per, per)].reshape(shard, pcols))
        return value

    def row_half(h):
        return slice(h * rsub, (h + 1) * rsub)

    y_far, y_near = [], [[None, None], [None, None]]
    for i, sign in enumerate((1, -1)):
        y_send[i, 0] = grad_term(2, row_half(i)).astype(BF16)
        y_far.append(links.copy(y_send.at[i, 0], y_recv.at[i, 0], place.along_tensor(sign)))
    got_dkv()
    both(s_k, "step")
    for i, sign in enumerate((1, -1)):
        y_send[i, 1] = grad_term(sign, row_half(1 - i)).astype(BF16)
        y_near[i][1 - i] = links.copy(y_send.at[i, 1], y_recv.at[i, 1], place.along_tensor(sign))
    fill()
    both(s_k, "step")
    fill()
    for i, sign in enumerate((1, -1)):
        value = grad_term(sign, row_half(i))
        y_far[i]()
        y_send[i, 2] = (value + y_recv[i, 0].astype(F32)).astype(BF16)
        y_near[i][i] = links.copy(y_send.at[i, 2], y_recv.at[i, 2], place.along_tensor(sign))
    fill()
    for _ in range(half - 2):
        both(s_k, "step")
        fill()
    home = [grad_term(0, row_half(h)) for h in range(2)]
    for h in range(2):
        hand_back(s_k, back_kv, back_kv_in, h)
    fill(len(later))
    for h in range(2):
        value = home[h]
        for i in range(2):
            y_near[i][h]()
            value += y_recv[i, 2 if h == i else 1].astype(F32)
        gt[row_half(h)] = value.astype(BF16)
    save(gt, gt_out)
    for wait in got_cyc:
        wait()
    for got in got_back:
        got()
    for i in range(2):
        cols = slice(i * hs, (i + 1) * hs)
        out_kv[:, i, :] = cyc_kv[:, i, :] + back_kv_in[:, cols].astype(F32)
    save(out_kv, out_kv_out)
    for p in range(groups):
        cols = slice(p * pcols, (p + 1) * pcols)
        out_q[:, cols] = cyc_q[:, cols] + back_q_in[p].astype(F32)
    save(out_q, out_q_out)
    links.drain()
    for made in saves:
        made.wait()


def layer(sizes, heads, pair, tok, wq, wkv, cot, acc_q, acc_kv, seg, span, counts):
    n_blk, n_seq, n_tensor = sizes
    chips = n_seq // 2
    half = chips // 2
    rows, width = tok.shape
    krows, qcols = wq.shape
    kcols = wkv.shape[1]
    hs = kcols // 2
    groups = heads // pair
    pcols = pair * hs
    n_keys = chips * rows
    sub, rsub = krows // 2, rows // 2
    hbm = pl.BlockSpec(memory_space=pl.ANY)
    vmem = pl.BlockSpec(memory_space=pltpu.VMEM)
    smem = pl.BlockSpec(memory_space=pltpu.SMEM)

    def weights(cols):
        return pltpu.VMEM((chips, 2, krows, cols), BF16)

    outs = [
        jax.ShapeDtypeStruct((rows, qcols), BF16),
        jax.ShapeDtypeStruct((rows, width), BF16),
        jax.ShapeDtypeStruct((krows, qcols), F32),
        jax.ShapeDtypeStruct((krows, 2, hs), F32),
    ]
    scratch = [pltpu.VMEM(out.shape, out.dtype) for out in outs] + [
        pltpu.VMEM((n_tensor, rows, width), BF16),
        pltpu.VMEM((chips, krows, 2 * rows), BF16),
        pltpu.VMEM((chips, krows, rows), BF16),
        pltpu.VMEM((groups, chips, 2, krows, pcols), BF16),
        weights(kcols),
        pltpu.VMEM((chips, 2, rows, kcols), BF16),
        pltpu.VMEM((rows, qcols), BF16),
        pltpu.VMEM((groups, rows, pcols), BF16),
        pltpu.VMEM((heads, hs, rows), BF16),
        pltpu.VMEM((heads, hs, rows), BF16),
        pltpu.VMEM((n_seq, rows, rows), F32),
        pltpu.VMEM((pair, 2, n_keys, rows), F32),
        pltpu.VMEM((pair, 2, n_keys, rows), BF16),
        pltpu.VMEM((pair, hs, rows), F32),
        pltpu.VMEM((pair, hs, rows), F32),
        pltpu.VMEM((2, n_keys, kcols), F32),
        pltpu.VMEM((chips, 2, rows, kcols), BF16),
        pltpu.VMEM((chips, rows, kcols), BF16),
        pltpu.VMEM((groups, 2 * rows, pcols), BF16),
        pltpu.VMEM((2 * rows, kcols), BF16),
        pltpu.VMEM((groups, 4, half, sub, pcols), BF16),
        pltpu.VMEM((groups, 4, half, sub, pcols), BF16),
        pltpu.VMEM((2, 4, half, sub, kcols), BF16),
        pltpu.VMEM((2, 4, half, sub, kcols), BF16),
        pltpu.VMEM((2, 3, rsub, width), BF16),
        pltpu.VMEM((2, 3, rsub, width), BF16),
        pltpu.VMEM((groups, krows, pcols), BF16),
        pltpu.VMEM((groups, krows, pcols), BF16),
        pltpu.VMEM((krows, kcols), BF16),
        pltpu.VMEM((krows, kcols), BF16),
        pltpu.VMEM((krows, qcols), F32),
        pltpu.VMEM((krows, 2, hs), F32),
        pltpu.SemaphoreType.DMA((256,)),
        pltpu.SemaphoreType.DMA((256,)),
        pltpu.SemaphoreType.DMA((6,)),
    ]
    return pl.pallas_call(
        functools.partial(layer_kernel, sizes, heads, pair, rows * n_seq),
        out_shape=outs,
        in_specs=[hbm] * 6 + [vmem, smem, smem],
        out_specs=[hbm] * 4,
        scratch_shapes=scratch,
        compiler_params=pltpu.CompilerParams(
            collective_id=0, has_side_effects=True, vmem_limit_bytes=62 * MIB
        ),
        name="layer",
    )(tok, wq, wkv, cot, acc_q, acc_kv, seg, span, counts)


def hand_over_kernel(count, *refs):
    sems = refs[-1]
    moves = [pltpu.make_async_copy(refs[i], refs[count + i], sems.at[i]) for i in range(count)]
    for move in moves:
        move.start()
    for move in moves:
        move.wait()


def hand_over(*arrays):
    count = len(arrays)
    hbm = pl.BlockSpec(memory_space=pl.ANY)
    return pl.pallas_call(
        functools.partial(hand_over_kernel, count),
        out_shape=[jax.ShapeDtypeStruct(a.shape, a.dtype) for a in arrays],
        in_specs=[pl.BlockSpec(memory_space=pltpu.VMEM)] * count,
        out_specs=[hbm] * count,
        scratch_shapes=[pltpu.SemaphoreType.DMA((count,))],
        compiler_params=pltpu.CompilerParams(vmem_limit_bytes=60 * MIB),
        name="hand_over",
    )(*arrays)


def on_device(
    sizes, tokens, w_query, w_keyval, accum_query, accum_keyval, cotangent, seg_ids, spans, counts
):
    krows, qcols = w_query.shape[1:]
    groups, kv_cols = w_keyval.shape[2:]
    kcols = groups * kv_cols
    context, grad_tokens, out_q, out_kv = layer(
        sizes, qcols // (kv_cols // 2), PAIR, tokens[0], w_query[0], w_keyval[0].reshape(krows, kcols),
        cotangent[0], accum_query[0], accum_keyval[0].reshape(krows, 2, kcols // 2), seg_ids, spans, counts,
    )
    context, grad_tokens, out_q, out_kv = hand_over(context, grad_tokens, out_q, out_kv)
    return context[None], grad_tokens[None], out_q[None], out_kv.reshape(w_keyval.shape)


def solution(mesh):
    sizes = (mesh.shape["blk"], mesh.shape["seq"], mesh.shape["tensor"])
    in_specs = (
        P("blk", "seq", "tensor"),
        P("blk", "seq", "tensor"),
        P("blk", "seq", "tensor", None),
        P("blk", "seq", "tensor"),
        P("blk", "seq", "tensor", None),
        P("blk", "seq", "tensor"),
        P("blk", None),
        P("blk", None, None),
        P("blk", None),
    )
    out_specs = (
        P("blk", "seq", "tensor"),
        P("blk", "seq", "tensor"),
        P("blk", "seq", "tensor"),
        P("blk", "seq", "tensor", None),
    )
    return jax.shard_map(
        functools.partial(on_device, sizes), mesh=mesh, in_specs=in_specs, out_specs=out_specs, check_vma=False
    )
```

time: 390 us -> 141 us (0.36)
  waiting for transfers between devices: 281 us -> 0 us
  Pallas kernels: 0 us -> 139 us
  matrix products: 56.1 us -> 0 us
  other arithmetic: 24.3 us -> 0 us
  between operations: 14.6 us -> 0.83 us
  starting transfers between devices: 6.04 us -> 0 us
  local copies, waits for them, and re-layouts: 6.95 us -> 1.34 us
    reduce_scatter x3 -> x0, waiting for transfers between devices: 175 us -> none  [the longest x1 71.1 us: on_device(): lax.psum_scatter(jnp.einsum('ic,ie->ce', full, dprojected, preferred_elem...]
    pallas_call x0 -> x2, Pallas kernels: none -> 139 us  [the longest x1 137 us: layer(): pl.pallas_call(functools.partial(layer_kernel, sizes, heads, pair, rows *...]
    all_gather x3 -> x0, waiting for transfers between devices: 96.7 us -> none  [the longest x1 48.5 us: on_device(): whole_w = lax.all_gather(part_w, 'seq', axis=0, tiled=True)]
    dot_general x9 -> x0, matrix products: 56.1 us -> none  [the longest x1 9.53 us: on_device(): jnp.einsum('igxd,jgd->gxij', upstream_gradient, value_rows, preferred_ele...]
    lt x1 -> x0, other arithmetic: 9.98 us -> none  [on_device(): kvalid = kpos % rows < owner]
    ppermute x5 -> x0, waiting for transfers between devices: 8.77 us -> none  [passed_along(): return lax.ppermute(block, axis, route)]
    ppermute x5 -> x0, starting transfers between devices: 5.79 us -> none  [passed_along(): return lax.ppermute(block, axis, route)]
  transfers between devices with their start and end apart: 11 -> 0, of which waited for: 7 -> 0; matrix products, arithmetic and copies ran while one was open for 9% -> 0% of each run, Pallas kernels for 0% -> 0%
where the time goes in v2:
time: 141 us
  Pallas kernels  139 us (99%)
    pallas_call x1, Pallas kernels, layer(): pl.pallas_call(functools.partial(layer_kernel, sizes, heads, pair, rows *...  137 us

profile of v2, /device:TPU:6, one launch (start us, length us, event | category | flops | bytes accessed | tf_op | source)
XLA Modules:
  0.0 141.2 jit_solution(3956015436820089160)
XLA Ops:
  0.6 0.0 copy-start
  0.6 0.7 copy-done
  1.3 0.7 copy.13.span
  2.0 136.6 %layer.1 = (bf16[256,512]{1,0:T(8,128)(2,1)}, bf16[256,1024]{1,0:T(8,128)(2,1)}, f32[256,512]{1,0:T(8,128)}, f32[256,2,128]{2,1,0:T(2,128)}) custom-call(bf16[256,1024]{1,0:T(8,128)(2,1)} %bitcast.10, bf16[256,512]{1,0:T(8,128)(2,1)} %bitcast.12, bf16[256,256]{1,0:T(8,128)(2,1)} %bitcast.15, bf16[256,512]{1,0:T(8,128)(2,1)} %bitcast.13, ...), custom_call_target="tpu_custom_call" | custom-call | tf_op jit(solution)/shard_map/layer/pallas_call | solution.py:600
  138.5 2.5 %hand_over.1 = (bf16[256,512]{1,0:T(8,128)(2,1)}, bf16[256,1024]{1,0:T(8,128)(2,1)}, f32[256,512]{1,0:T(8,128)}, f32[256,2,128]{2,1,0:T(2,128)}) custom-call(bf16[256,512]{1,0:T(8,128)(2,1)} %get-tuple-element.12.refs_0_, bf16[256,1024]{1,0:T(8,128)(2,1)} %get-tuple-element.13.refs_1_, f32[256,512]{1,0:T(8,128)} %get-tuple-element.14.refs_2_, ...), custom_call_target="tpu_custom_call" | custom-call | tf_op jit(solution)/shard_map/hand_over/pallas_call | solution.py:625
Async XLA Ops:
  0.6 0.7 copy-start

commit v3 on v2

--- a/solution.py
+++ b/solution.py
@@ -14,7 +14,7 @@
 LOG2E = 1.4426950408889634
 MASKED = -1e30
 PAIR = 2
-FILLS = (0, 1, 2, 0, 2, 1, 0, 2, 0, 2, 1, 0, 0, 1, 2, 1, 1, 0, 2, 5, 0, 1, 1, 1, 1, 2, 2, 1, 2, 2, 1, 0, 0, 1, 2)
+FILLS = (0, 1, 2, 0, 2, 1, 0, 2, 1, 2, 1, 0, 1, 0, 2, 0, 1, 1, 1, 2, 0, 1, 1, 1, 1, 2, 2, 2, 1, 2, 1, 0, 0, 1, 2)
 
 
 def matmul(a, b):
@@ -36,6 +36,9 @@
     def at(self, distance):
         return lax.rem(self.chip + distance + self.chips, self.chips)
 
+    def slot(self, distance):
+        return (distance - self.chips // 4) % self.chips
+
     def along_seq(self, distance):
         return {"seq": 2 * self.at(distance) + self.core}
 
@@ -55,7 +58,7 @@
             others += [self.along_seq(sign), self.along_blk(sign), self.along_tensor(sign)]
         for other in others:
             pl.semaphore_signal(barrier, inc=1, device_id=other, device_id_type=MESH)
-        pl.semaphore_wait(barrier, len(others))
+        return lambda: pl.semaphore_wait(barrier, len(others))
 
 
 class Links:
@@ -85,12 +88,14 @@
 
 
 class Gather:
-    def __init__(self, place, links, buf):
+    def __init__(self, place, links, buf, by_distance=False):
         self.place, self.links, self.buf = place, links, buf
+        self.by_distance = by_distance
+        self.slot = place.slot if by_distance else place.at
         self.half = place.chips // 2
         sub = buf.shape[2] // 2
         self.parts = (pl.ds(0, sub), pl.ds(sub, sub))
-        self.done, self.waits, self.shares, self.finished = [0, 0], [None, None], [], False
+        self.done, self.waits, self.shares, self.finished, self.taken = [0, 0], [None, None], [], False, 0
 
     def start(self, h):
         place, c = self.place, self.place.core
@@ -99,14 +104,15 @@
         for i, sign in enumerate((1, -1)):
             if step == self.half and i != h:
                 continue
-            src = self.buf.at[place.at(-sign * (step - 1)), c, self.parts[h]]
-            lands = self.buf.at[place.at(-sign * step), c, self.parts[h]]
-            self.waits[h].append(self.links.copy(src, src, place.along_seq(sign), lands))
+            src = self.buf.at[self.slot(-sign * (step - 1)), c, self.parts[h]]
+            lands = self.buf.at[self.slot(-sign * step), c, self.parts[h]]
+            there = lands if self.by_distance else src
+            self.waits[h].append(self.links.copy(src, there, place.along_seq(sign), lands))
 
     def share(self, distance):
         place = self.place
-        src = self.buf.at[place.at(distance), place.core]
-        lands = self.buf.at[place.at(distance), 1 - place.core]
+        src = self.buf.at[self.slot(distance), place.core]
+        lands = self.buf.at[self.slot(distance), 1 - place.core]
         self.shares.append(self.links.copy(src, src, place.sibling, lands))
 
     def advance(self, h):
@@ -120,8 +126,10 @@
             for distance in (step, -step) if step < self.half else (step,):
                 self.share(distance)
 
-    def collect(self):
-        for wait in self.shares:
+    def collect(self, count=None):
+        shares = self.shares[self.taken:count]
+        self.taken += len(shares)
+        for wait in shares:
             wait()
 
 
@@ -165,8 +173,8 @@
 def layer_kernel(
     sizes, heads, pair, total, tok, wq, wkv, cot, acc_q, acc_kv, seg, span, counts,
     ctx_out, gt_out, out_q_out, out_kv_out,
-    ctx, gt, out_q, out_kv, xb, x2t, xts, wqbs, wkvb, kvb, cotb, qb, qt, ut, bias, s_buf, e_buf, o_acc, dq_acc, dk_acc, dkvb, sib,
-    dq2, dkv2, rq_send, rq_recv, r_send, r_recv, y_send, y_recv, back_q, back_q_in, back_kv, back_kv_in,
+    ctx, gt, out_q, out_kv, xb, x2, wqbs, wkvb, kvb, cotb, qb, qt, ut, bias, s_buf, e_buf, o_acc, dq_acc, dk_acc, dkvb, sib,
+    dq, dqt, dkv, dkvt, gt_sum, rq_send, rq_recv, r_send, r_recv, y_send, y_recv, back_q, back_q_in, back_kv, back_kv_in,
     cyc_q, cyc_kv, send, recv, local,
 ):
     place = Place(*sizes)
@@ -187,7 +195,33 @@
     own_tok.start()
     own_cot = pltpu.make_async_copy(cot, cotb, local.at[1])
     own_cot.start()
-    place.greet()
+    greeted = place.greet()
+
+    me = 2 * place.chip + c
+    slots = span.shape[2]
+    seg_all = seg[...]
+    seg_q = seg[:, pl.ds(pl.multiple_of(me * rows, rows), rows)]
+    lane = lax.broadcasted_iota(jnp.int32, (1, rows), 1)
+    qpos = me * rows + lane
+    lo = jnp.zeros((1, rows), jnp.int32)
+    hi = jnp.zeros((1, rows), jnp.int32)
+    begin = jnp.zeros((1, 1), jnp.int32)
+    for s in range(slots):
+        end = jnp.sum((seg_all <= s).astype(F32), axis=1, keepdims=True).astype(jnp.int32)
+        first, last = span[0, 0, s], span[0, 1, s]
+        here = seg_q == s
+        inside = (qpos >= first) & (qpos < last)
+        lo = jnp.where(here, begin, lo)
+        hi = jnp.where(here, jnp.where(inside, jnp.minimum(last, end), qpos + 1), hi)
+        begin = end
+    valid_t = lane < counts[0, me]
+    row = lax.broadcasted_iota(jnp.int32, (rows, rows), 0)
+    for d in range(chips):
+        for core in range(2):
+            b = 2 * place.at(d) + core
+            low, high = lo - b * rows, jnp.minimum(hi - b * rows, counts[0, b])
+            bias[2 * place.slot(d) + core] = jnp.where((row >= low) & (row < high), 0.0, MASKED)
+    greeted()
 
     ahead = place.along_blk(1)
     halves = (pl.ds(0, sub), pl.ds(sub, sub))
@@ -208,7 +242,7 @@
 
     g_wkv = Gather(place, links, wkvb)
     g_wq = [Gather(place, links, buf) for buf in wqb]
-    g_kv = Gather(place, links, kvb)
+    g_kv = Gather(place, links, kvb, by_distance=True)
 
     later = []
 
@@ -250,35 +284,8 @@
         ))
     fill()
 
-    me = 2 * place.chip + c
-    slots = span.shape[1]
-    seg_all = seg[...]
-    seg_q = seg[:, pl.ds(pl.multiple_of(me * rows, rows), rows)]
-    lane = lax.broadcasted_iota(jnp.int32, (1, rows), 1)
-    qpos = me * rows + lane
-    lo = jnp.zeros((1, rows), jnp.int32)
-    hi = jnp.zeros((1, rows), jnp.int32)
-    begin = jnp.zeros((1, 1), jnp.int32)
-    for s in range(slots):
-        end = jnp.sum((seg_all <= s).astype(F32), axis=1, keepdims=True).astype(jnp.int32)
-        first, last = span[0, s, 0], span[0, s, 1]
-        here = seg_q == s
-        inside = (qpos >= first) & (qpos < last)
-        lo = jnp.where(here, begin, lo)
-        hi = jnp.where(here, jnp.where(inside, jnp.minimum(last, end), qpos + 1), hi)
-        begin = end
-    valid_t = lane < counts[0, me]
-    row = lax.broadcasted_iota(jnp.int32, (rows, 1), 0)
-
-    def mask(blocks):
-        for b in blocks:
-            j = jnp.where(row < counts[0, b], b * rows + row, -1)
-            bias[b] = jnp.where((j >= lo) & (j < hi), 0.0, MASKED)
-
-    mask(range(chips))
     both(g_wkv)
     fill()
-    mask(range(chips, 2 * chips))
     both(g_wkv)
     fill()
     own_cot.wait()
@@ -302,7 +309,7 @@
             out = term if out is None else out + term
         return out.astype(BF16)
 
-    kvb[place.chip, c] = project(wkvb)
+    kvb[place.slot(0), c] = project(wkvb)
     both(g_kv, "start")
     g_kv.share(0)
     fill()
@@ -316,15 +323,16 @@
 
     x_got = []
 
-    def turn(t):
+    def own_columns(t):
         for p in range(per):
-            z = t * per + p
             mine = pl.ds(pl.multiple_of((2 * p + c) * krows, krows), krows)
+            x2[t * per + p, :rows] = xb[t, :, mine]
+
+    def share_columns():
+        for z in range(chips):
+            t, p = z // per, z % per
             other = pl.ds(pl.multiple_of((2 * p + 1 - c) * krows, krows), krows)
-            x2t[z, :, :rows] = xb[t, :, mine].T
-            xts[z] = xb[t, :, other].T
-        z = pl.ds(t * per, per)
-        x_got.append(links.copy(xts.at[z], x2t.at[z, :, pl.ds(rows, rows)], place.sibling))
+            x_got.append(links.copy(xb.at[t, :, other], x2.at[z, pl.ds(rows, rows)], place.sibling))
 
     def queries(p):
         while not g_wq[p].finished:
@@ -334,43 +342,49 @@
         for i in range(pair):
             qt[pair * p + i] = qb[p, :, i * hs:(i + 1) * hs].T
 
-    turns = list(range(n_tensor))
+    def rows8(x, op):
+        return op(x.reshape(x.shape[0] // 8, 8, rows), axis=0)
+
+    scale = hs ** -0.5
+    n_keys = chips * rows
+
+    def look(p, part, tops):
+        z = slice(part * half, (part + 1) * half)
+        b = slice(part * chips, (part + 1) * chips)
+        key = kvb[z, :, :, :hs].reshape(n_keys, hs)
+        found = []
+        for i in range(pair):
+            s = matmul(key, qt[pair * p + i]) + bias[b].reshape(n_keys, rows)
+            s_buf[i, part] = s
+            found.append(jnp.maximum(tops[i], rows8(s, jnp.max)))
+        return found
+
     for step in range(half):
-        for _ in range(2 if step == 1 else 1):
-            if turns:
-                turn(turns.pop(0))
         if step == half - 1:
             queries(0)
+            g_kv.collect(2 * half - 3)
+            tops = look(0, 1, [jnp.full((8, rows), MASKED, F32)] * pair)
+        else:
+            for t in range(step, n_tensor, half - 1):
+                own_columns(t)
         fill()
         both(g_kv)
         fill()
-    while turns:
-        turn(turns.pop(0))
     g_kv.collect()
-
-    def rows8(x, op):
-        return op(x.reshape(x.shape[0] // 8, 8, rows), axis=0)
-
-    scale = hs ** -0.5
-    n_keys = chips * rows
-
-    def attend(p):
+    share_columns()
+
+    def attend(p, tops=None):
         last = p == groups - 1
 
         def tick(enough=False):
             if not enough:
                 fill()
 
-        tops = [jnp.full((8, rows), MASKED, F32)] * pair
-        for part in range(2):
-            z = slice(part * half, (part + 1) * half)
-            b = slice(part * chips, (part + 1) * chips)
-            for i in range(pair):
-                key = kvb[z, :, :, :hs].reshape(n_keys, hs)
-                s = matmul(key, qt[pair * p + i]) + bias[b].reshape(n_keys, rows)
-                s_buf[i, part] = s
-                tops[i] = jnp.maximum(tops[i], rows8(s, jnp.max))
-            tick()
+        if tops is None:
+            tops = look(p, 1, [jnp.full((8, rows), MASKED, F32)] * pair)
+        tick()
+        tops = look(p, 0, tops)
+        tick()
         tops = [jnp.max(t, axis=0, keepdims=True) * (scale * LOG2E) for t in tops]
         sums = [jnp.zeros((8, rows), F32)] * pair
         for part in range(2):
@@ -420,9 +434,11 @@
                 dk_acc[part, :, hs:] = dval
             tick(part == 1)
         for i in range(pair):
-            dq2[p, :rows, i * hs:(i + 1) * hs] = (dq_acc[i] * scale).T.astype(BF16)
-        mine = dq2.at[p, pl.ds(0, rows)]
-        got_dq = links.copy(mine, dq2.at[p, pl.ds(rows, rows)], place.sibling)
+            dqt[p, i * hs:(i + 1) * hs, :rows] = (dq_acc[i] * scale).astype(BF16)
+        mine = dqt.at[p, :, pl.ds(0, rows)]
+        got_dq = links.copy(mine, dqt.at[p, :, pl.ds(rows, rows)], place.sibling)
+        for i in range(pair):
+            dq[p, :, i * hs:(i + 1) * hs] = (dq_acc[i] * scale).T.astype(BF16)
 
         def first_step():
             got_dq()
@@ -439,25 +455,25 @@
     exchanged = []
 
     def fresh_term(grads):
-        return lambda d, part: matmul(x2t[place.at(d), part], grads[...])
+        return lambda d, part: matmul(grads[part], x2[place.at(d)])
 
     def kv_term(d, part):
-        here = place.at(d)
+        here = place.slot(d)
         return dkvb[here, c, part].astype(F32) + sib[here, part].astype(F32)
 
     s_q = [
-        Scatter(place, links, fresh_term(dq2.at[p]), rq_send.at[p], rq_recv.at[p]) for p in range(groups)
+        Scatter(place, links, fresh_term(dqt.at[p]), rq_send.at[p], rq_recv.at[p]) for p in range(groups)
     ]
     s_kv = Scatter(place, links, kv_term, r_send.at[0], r_recv.at[0])
-    s_k = Scatter(place, links, fresh_term(dkv2), r_send.at[1], r_recv.at[1])
-    got_back = []
+    s_k = Scatter(place, links, fresh_term(dkvt), r_send.at[1], r_recv.at[1])
+    got_back = {}
 
     def hand_back(scatter, out, came, h):
         part = pl.ds(h * sub, sub)
         out[part] = (scatter.result(h) / total).astype(BF16)
-        got_back.append(links.copy(out.at[part], came.at[part], place.along_blk(-1)))
-
-    attend(0)
+        got_back[scatter, h] = links.copy(out.at[part], came.at[part], place.along_blk(-1))
+
+    attend(0, tops)
     for wait in x_got:
         wait()
     for p in range(1, groups):
@@ -465,54 +481,65 @@
         fill()
         attend(p)
     save(ctx, ctx_out)
-    for wait in exchanged:
-        wait()
-    for _ in range(half):
+    shares = (2, 1, -1, 0)
+    shard = 2 * per * krows
+
+    def add_queries(i):
+        t = place.tensor_at(shares[i])
+        value = None
+        for p in range(groups):
+            term = matmul_t(dq[p], wqb[p][pl.ds(t * per, per)].reshape(shard, pcols))
+            value = term if value is None else value + term
+        gt_sum[i] = value
+
+    def add_keyval(i):
+        t = place.tensor_at(shares[i])
+        gt_sum[i] += matmul_t(dkv[...], wkvb[pl.ds(t * per, per)].reshape(shard, kcols))
+
+    for step in range(half):
+        if step < 2:
+            exchanged[step]()
         both(s_kv, "step")
         fill()
+        for i in range(step, len(shares), half):
+            add_queries(i)
     for h in range(2):
-        dkv2[h * rsub:(h + 1) * rsub] = s_kv.result(h).astype(BF16)
-    got_dkv = links.copy(dkv2.at[pl.ds(0, rows)], dkv2.at[pl.ds(rows, rows)], place.sibling)
-
-    shard = 2 * per * krows
-
-    def grad_term(distance, part):
-        t = place.tensor_at(distance)
-        value = matmul_t(dkv2[part], wkvb[pl.ds(t * per, per)].reshape(shard, kcols))
-        for p in range(groups):
-            value += matmul_t(dq2[p, part], wqb[p][pl.ds(t * per, per)].reshape(shard, pcols))
-        return value
+        value = s_kv.result(h)
+        dkv[h * rsub:(h + 1) * rsub] = value.astype(BF16)
+        dkvt[:, h * rsub:(h + 1) * rsub] = value.T.astype(BF16)
+    got_dkv = links.copy(dkvt.at[:, pl.ds(0, rows)], dkvt.at[:, pl.ds(rows, rows)], place.sibling)
 
     def row_half(h):
         return slice(h * rsub, (h + 1) * rsub)
 
     y_far, y_near = [], [[None, None], [None, None]]
+    add_keyval(0)
     for i, sign in enumerate((1, -1)):
-        y_send[i, 0] = grad_term(2, row_half(i)).astype(BF16)
+        y_send[i, 0] = gt_sum[0, row_half(i)].astype(BF16)
         y_far.append(links.copy(y_send.at[i, 0], y_recv.at[i, 0], place.along_tensor(sign)))
     got_dkv()
     both(s_k, "step")
     for i, sign in enumerate((1, -1)):
-        y_send[i, 1] = grad_term(sign, row_half(1 - i)).astype(BF16)
+        add_keyval(1 + i)
+        y_send[i, 1] = gt_sum[1 + i, row_half(1 - i)].astype(BF16)
         y_near[i][1 - i] = links.copy(y_send.at[i, 1], y_recv.at[i, 1], place.along_tensor(sign))
     fill()
     both(s_k, "step")
     fill()
     for i, sign in enumerate((1, -1)):
-        value = grad_term(sign, row_half(i))
         y_far[i]()
-        y_send[i, 2] = (value + y_recv[i, 0].astype(F32)).astype(BF16)
+        y_send[i, 2] = (gt_sum[1 + i, row_half(i)] + y_recv[i, 0].astype(F32)).astype(BF16)
         y_near[i][i] = links.copy(y_send.at[i, 2], y_recv.at[i, 2], place.along_tensor(sign))
+    add_keyval(3)
     fill()
     for _ in range(half - 2):
         both(s_k, "step")
         fill()
-    home = [grad_term(0, row_half(h)) for h in range(2)]
     for h in range(2):
         hand_back(s_k, back_kv, back_kv_in, h)
     fill(len(later))
     for h in range(2):
-        value = home[h]
+        value = gt_sum[3, row_half(h)]
         for i in range(2):
             y_near[i][h]()
             value += y_recv[i, 2 if h == i else 1].astype(F32)
@@ -520,16 +547,16 @@
     save(gt, gt_out)
     for wait in got_cyc:
         wait()
-    for got in got_back:
-        got()
-    for i in range(2):
-        cols = slice(i * hs, (i + 1) * hs)
-        out_kv[:, i, :] = cyc_kv[:, i, :] + back_kv_in[:, cols].astype(F32)
+    for p in range(groups):
+        for h in range(2):
+            got_back[s_q[p], h]()
+        cols = slice(p * pcols, (p + 1) * pcols)
+        out_q[:, cols] = cyc_q[:, cols] + back_q_in[p].astype(F32).T
+    save(out_q, out_q_out)
+    for h in range(2):
+        got_back[s_k, h]()
+        out_kv[:, h, :] = cyc_kv[:, h, :] + back_kv_in[h * hs:(h + 1) * hs].astype(F32).T
     save(out_kv, out_kv_out)
-    for p in range(groups):
-        cols = slice(p * pcols, (p + 1) * pcols)
-        out_q[:, cols] = cyc_q[:, cols] + back_q_in[p].astype(F32)
-    save(out_q, out_q_out)
     links.drain()
     for made in saves:
         made.wait()
@@ -562,8 +589,7 @@
     ]
     scratch = [pltpu.VMEM(out.shape, out.dtype) for out in outs] + [
         pltpu.VMEM((n_tensor, rows, width), BF16),
-        pltpu.VMEM((chips, krows, 2 * rows), BF16),
-        pltpu.VMEM((chips, krows, rows), BF16),
+        pltpu.VMEM((chips, 2 * rows, krows), BF16),
         pltpu.VMEM((groups, chips, 2, krows, pcols), BF16),
         weights(kcols),
         pltpu.VMEM((chips, 2, rows, kcols), BF16),
@@ -579,18 +605,21 @@
         pltpu.VMEM((2, n_keys, kcols), F32),
         pltpu.VMEM((chips, 2, rows, kcols), BF16),
         pltpu.VMEM((chips, rows, kcols), BF16),
-        pltpu.VMEM((groups, 2 * rows, pcols), BF16),
-        pltpu.VMEM((2 * rows, kcols), BF16),
+        pltpu.VMEM((groups, rows, pcols), BF16),
+        pltpu.VMEM((groups, pcols, 2 * rows), BF16),
+        pltpu.VMEM((rows, kcols), BF16),
+        pltpu.VMEM((kcols, 2 * rows), BF16),
+        pltpu.VMEM((4, rows, width), F32),
         pltpu.VMEM((groups, 4, half, sub, pcols), BF16),
         pltpu.VMEM((groups, 4, half, sub, pcols), BF16),
         pltpu.VMEM((2, 4, half, sub, kcols), BF16),
         pltpu.VMEM((2, 4, half, sub, kcols), BF16),
         pltpu.VMEM((2, 3, rsub, width), BF16),
         pltpu.VMEM((2, 3, rsub, width), BF16),
-        pltpu.VMEM((groups, krows, pcols), BF16),
-        pltpu.VMEM((groups, krows, pcols), BF16),
-        pltpu.VMEM((krows, kcols), BF16),
-        pltpu.VMEM((krows, kcols), BF16),
+        pltpu.VMEM((groups, pcols, krows), BF16),
+        pltpu.VMEM((groups, pcols, krows), BF16),
+        pltpu.VMEM((kcols, krows), BF16),
+        pltpu.VMEM((kcols, krows), BF16),
         pltpu.VMEM((krows, qcols), F32),
         pltpu.VMEM((krows, 2, hs), F32),
         pltpu.SemaphoreType.DMA((256,)),
@@ -641,7 +670,7 @@
     kcols = groups * kv_cols
     context, grad_tokens, out_q, out_kv = layer(
         sizes, qcols // (kv_cols // 2), PAIR, tokens[0], w_query[0], w_keyval[0].reshape(krows, kcols),
-        cotangent[0], accum_query[0], accum_keyval[0].reshape(krows, 2, kcols // 2), seg_ids, spans, counts,
+        cotangent[0], accum_query[0], accum_keyval[0].reshape(krows, 2, kcols // 2), seg_ids, jnp.swapaxes(spans, 1, 2), counts,
     )
     context, grad_tokens, out_q, out_kv = hand_over(context, grad_tokens, out_q, out_kv)
     return context[None], grad_tokens[None], out_q[None], out_kv.reshape(w_keyval.shape)

time: 141 us -> 136 us (0.965)
  Pallas kernels: 139 us -> 135 us
    pallas_call x1, Pallas kernels: 137 us -> 133 us  [layer(): pl.pallas_call(functools.partial(layer_kernel, sizes, heads, pair, rows *...]
where the time goes in v3:
time: 136 us
  Pallas kernels  135 us (99%)
    pallas_call x1, Pallas kernels, layer(): pl.pallas_call(functools.partial(layer_kernel, sizes, heads, pair, rows *...  133 us

profile of v3, /device:TPU:6, one launch (start us, length us, event | category | flops | bytes accessed | tf_op | source)
XLA Modules:
  0.0 136.1 jit_solution(9422290748579549771)
XLA Ops:
  0.6 132.7 %layer.1 = (bf16[256,512]{1,0:T(8,128)(2,1)}, bf16[256,1024]{1,0:T(8,128)(2,1)}, f32[256,512]{1,0:T(8,128)}, f32[256,2,128]{2,1,0:T(2,128)}) custom-call(bf16[256,1024]{1,0:T(8,128)(2,1)} %bitcast.11, bf16[256,512]{1,0:T(8,128)(2,1)} %bitcast.13, bf16[256,256]{1,0:T(8,128)(2,1)} %bitcast.16, bf16[256,512]{1,0:T(8,128)(2,1)} %bitcast.14, ...), custom_call_target="tpu_custom_call" | custom-call | tf_op jit(solution)/shard_map/layer/pallas_call | solution.py:629
  133.4 2.5 %hand_over.1 = (bf16[256,512]{1,0:T(8,128)(2,1)}, bf16[256,1024]{1,0:T(8,128)(2,1)}, f32[256,512]{1,0:T(8,128)}, f32[256,2,128]{2,1,0:T(2,128)}) custom-call(bf16[256,512]{1,0:T(8,128)(2,1)} %get-tuple-element.12.refs_0_, bf16[256,1024]{1,0:T(8,128)(2,1)} %get-tuple-element.13.refs_1_, f32[256,512]{1,0:T(8,128)} %get-tuple-element.14.refs_2_, ...), custom_call_target="tpu_custom_call" | custom-call | tf_op jit(solution)/shard_map/hand_over/pallas_call | solution.py:654

commit v4 on v3

--- a/solution.py
+++ b/solution.py
@@ -14,7 +14,7 @@
 LOG2E = 1.4426950408889634
 MASKED = -1e30
 PAIR = 2
-FILLS = (0, 1, 2, 0, 2, 1, 0, 2, 1, 2, 1, 0, 1, 0, 2, 0, 1, 1, 1, 2, 0, 1, 1, 1, 1, 2, 2, 2, 1, 2, 1, 0, 0, 1, 2)
+FILLS = (0, 1, 2, 0, 2, 1, 0, 2, 1, 2, 1, 0, 1, 0, 2, 0, 1, 1, 1, 2, 1, 1, 1, 1, 1, 2, 2, 2, 2, 1, 1, 1, 1, 1, 1)
 
 
 def matmul(a, b):
@@ -640,12 +640,16 @@
 
 
 def hand_over_kernel(count, *refs):
-    sems = refs[-1]
-    moves = [pltpu.make_async_copy(refs[i], refs[count + i], sems.at[i]) for i in range(count)]
-    for move in moves:
-        move.start()
-    for move in moves:
-        move.wait()
+    arrays, results, held, sems = refs[:count], refs[count:2 * count], refs[2 * count:-1], refs[-1]
+    comes = [pltpu.make_async_copy(arrays[i], held[i], sems.at[0, i]) for i in range(count)]
+    goes = [pltpu.make_async_copy(held[i], results[i], sems.at[1, i]) for i in range(count)]
+    for come in comes:
+        come.start()
+    for come, go in zip(comes, goes):
+        come.wait()
+        go.start()
+    for go in goes:
+        go.wait()
 
 
 def hand_over(*arrays):
@@ -654,9 +658,9 @@
     return pl.pallas_call(
         functools.partial(hand_over_kernel, count),
         out_shape=[jax.ShapeDtypeStruct(a.shape, a.dtype) for a in arrays],
-        in_specs=[pl.BlockSpec(memory_space=pltpu.VMEM)] * count,
+        in_specs=[hbm] * count,
         out_specs=[hbm] * count,
-        scratch_shapes=[pltpu.SemaphoreType.DMA((count,))],
+        scratch_shapes=[pltpu.VMEM(a.shape, a.dtype) for a in arrays] + [pltpu.SemaphoreType.DMA((2, count))],
         compiler_params=pltpu.CompilerParams(vmem_limit_bytes=60 * MIB),
         name="hand_over",
     )(*arrays)

time: 136 us -> 136 us (level)
  no operation moved by 1% of the time
where the time goes in v4:
time: 136 us
  Pallas kernels  135 us (99%)
    pallas_call x1, Pallas kernels, layer(): pl.pallas_call(functools.partial(layer_kernel, sizes, heads, pair, rows *...  133 us

profile of v4, /device:TPU:6, one launch (start us, length us, event | category | flops | bytes accessed | tf_op | source)
XLA Modules:
  0.0 135.6 jit_solution(14962035708633241038)
XLA Ops:
  0.6 132.5 %layer.1 = (bf16[256,512]{1,0:T(8,128)(2,1)}, bf16[256,1024]{1,0:T(8,128)(2,1)}, f32[256,512]{1,0:T(8,128)}, f32[256,2,128]{2,1,0:T(2,128)}) custom-call(bf16[256,1024]{1,0:T(8,128)(2,1)} %bitcast.11, bf16[256,512]{1,0:T(8,128)(2,1)} %bitcast.13, bf16[256,256]{1,0:T(8,128)(2,1)} %bitcast.16, bf16[256,512]{1,0:T(8,128)(2,1)} %bitcast.14, ...), custom_call_target="tpu_custom_call" | custom-call | tf_op jit(solution)/shard_map/layer/pallas_call | solution.py:629
  133.2 2.2 %hand_over.1 = (bf16[256,512]{1,0:T(8,128)(2,1)}, bf16[256,1024]{1,0:T(8,128)(2,1)}, f32[256,512]{1,0:T(8,128)}, f32[256,2,128]{2,1,0:T(2,128)}) custom-call(bf16[256,512]{1,0:T(8,128)(2,1)} %get-tuple-element.12.refs_0_, bf16[256,1024]{1,0:T(8,128)(2,1)} %get-tuple-element.13.refs_1_, f32[256,512]{1,0:T(8,128)} %get-tuple-element.14.refs_2_, ...), custom_call_target="tpu_custom_call" | custom-call | tf_op jit(solution)/shard_map/hand_over/pallas_call | solution.py:658
